TPU v7x, 32 devices: a whole 2x2x4 slice. The times are simulated.
32 devices in a mesh: gx: 8 (over z, y), gy: 4 (over x, core).
Axes of the slice: x: 2, y: 2, z: 4, core: 2. Of those that a mesh axis runs over, the one named last changes fastest.
Arguments:
- tokens: bfloat16 [128, 256, 768], P(('gx', 'gy')), may hold values from -6 to 6
- segment_ids: int32 [128, 256], P(('gx', 'gy')), may hold values from 0 to 7, never falling along the last dimension, each value on 1 to 64 neighbouring positions
- pad_mask: int32 [128, 256], P(('gx', 'gy')), may hold values 0 or 1
- w_qkv: bfloat16 [768, 2304], P(('gx', 'gy')), may hold values from -0.21875 to 0.21875
- w_out: bfloat16 [768, 768], P(('gx', 'gy')), may hold values from -0.875 to 0.875
- w_up: bfloat16 [768, 3072], P(('gx', 'gy')), may hold values from -0.21875 to 0.21875
- w_down: bfloat16 [3072, 768], P(('gx', 'gy')), may hold values from -0.109375 to 0.109375
- gain_one: bfloat16 [768], P(('gx', 'gy')), may hold values from 0.099609375 to 1.8984375
- shift_one: bfloat16 [768], P(('gx', 'gy')), may hold values from -3 to 3
- bias_query: bfloat16 [768], P(('gx', 'gy')), may hold values from -3 to 3
- bias_value: bfloat16 [768], P(('gx', 'gy')), may hold values from -3 to 3
- bias_out: bfloat16 [768], P(('gx', 'gy')), may hold values from -2 to 2
- gain_two: bfloat16 [768], P(('gx', 'gy')), may hold values from 0.099609375 to 1.8984375
- shift_two: bfloat16 [768], P(('gx', 'gy')), may hold values from -3 to 3
- bias_up: bfloat16 [3072], P(('gx', 'gy')), may hold values from -3 to 3
- bias_down: bfloat16 [768], P(('gx', 'gy')), may hold values from -2 to 2
- cotangent: bfloat16 [128, 256, 768], P(('gx', 'gy')), may hold values from -6 to 6
Outputs:
- output: bfloat16 [128, 256, 768], P(('gx', 'gy'))
- grad_tokens: float32 [128, 256, 768], P(('gx', 'gy'))
- grad_w_qkv: float32 [768, 2304], P(('gx', 'gy'))
- grad_w_out: float32 [768, 768], P(('gx', 'gy'))
- grad_w_up: float32 [768, 3072], P(('gx', 'gy'))
- grad_w_down: float32 [3072, 768], P(('gx', 'gy'))
- grad_gain_one: float32 [768], P(('gx', 'gy'))
- grad_shift_one: float32 [768], P(('gx', 'gy'))
- grad_bias_query: float32 [768], P(('gx', 'gy'))
- grad_bias_value: float32 [768], P(('gx', 'gy'))
- grad_bias_out: float32 [768], P(('gx', 'gy'))
- grad_gain_two: float32 [768], P(('gx', 'gy'))
- grad_shift_two: float32 [768], P(('gx', 'gy'))
- grad_bias_up: float32 [3072], P(('gx', 'gy'))
- grad_bias_down: float32 [768], P(('gx', 'gy'))
Inputs may be any that keep to these rules, and one draw needn't show every extreme that they name: `segment_ids`: within a row the numbers never fall and each caption takes 1 to 64 positions, one exactly 64.
All inputs are finite; a program needn't handle non-finite values. No bound on the sum of `pad_mask` on one device may be relied on, other than what follows from the above.
Results may differ from a plain program's by a relative error of at most 0.012.
Values may be sent and summed in bfloat16 or wider, within the bound.
No kernel may reach another device: no remote copies, remote signals or barrier semaphores. Data moves between devices by JAX's collectives and lax.ppermute only.
A program may use at most 192 MiB of HBM per device.

v0:
```python
import math

import jax
import jax.numpy as jnp
from jax import lax
from jax.sharding import PartitionSpec as P

HEADS = 12
HDIM = 64


def layer_norm(values, gain, shift):
    centre = values - jnp.mean(values, axis=-1, keepdims=True)
    spread = jnp.mean(centre * centre, axis=-1, keepdims=True)
    return centre * lax.rsqrt(spread + 1e-06) * gain + shift


def smooth_gate(values):
    return jax.nn.gelu(values, approximate=True)


def attend_mask(segment_ids, pad_mask):
    length = segment_ids.shape[-1]
    positions = jnp.arange(length)
    same = segment_ids[:, :, None] == segment_ids[:, None, :]
    real = pad_mask[:, None, :] == 1
    itself = positions[:, None] == positions[None, :]
    return same & (real | itself[None])


def outer_sum(left, right):
    return lax.dot_general(
        left, right, (((0,), (0,)), ((), ())), preferred_element_type=jnp.float32
    )


def against(left, matrix):
    return lax.dot_general(
        left, matrix, (((1,), (1,)), ((), ())), preferred_element_type=jnp.float32
    )


def score_block(query_part, key_part, allowed):
    raw = jnp.einsum("rqhe,rkhe->rhqk", query_part, key_part, preferred_element_type=jnp.float32)
    raw = raw * (1.0 / math.sqrt(HDIM))
    return jnp.where(allowed[:, None], raw, -1e30)


def collect(
    w_qkv,
    w_out,
    w_up,
    w_down,
    gain_one,
    shift_one,
    bias_query,
    bias_value,
    bias_out,
    gain_two,
    shift_two,
    bias_up,
    bias_down,
):
    return (
        lax.all_gather(w_qkv, ("gx", "gy"), axis=0, tiled=True),
        lax.all_gather(w_out, ("gx", "gy"), axis=0, tiled=True),
        lax.all_gather(w_up, ("gx", "gy"), axis=0, tiled=True),
        lax.all_gather(w_down, ("gx", "gy"), axis=0, tiled=True),
        lax.all_gather(gain_one, ("gx", "gy"), axis=0, tiled=True),
        lax.all_gather(shift_one, ("gx", "gy"), axis=0, tiled=True),
        lax.all_gather(bias_query, ("gx", "gy"), axis=0, tiled=True),
        lax.all_gather(bias_value, ("gx", "gy"), axis=0, tiled=True),
        lax.all_gather(bias_out, ("gx", "gy"), axis=0, tiled=True),
        lax.all_gather(gain_two, ("gx", "gy"), axis=0, tiled=True),
        lax.all_gather(shift_two, ("gx", "gy"), axis=0, tiled=True),
        lax.all_gather(bias_up, ("gx", "gy"), axis=0, tiled=True),
        lax.all_gather(bias_down, ("gx", "gy"), axis=0, tiled=True),
    )


def on_device(
    tokens,
    segment_ids,
    pad_mask,
    w_qkv,
    w_out,
    w_up,
    w_down,
    gain_one,
    shift_one,
    bias_query,
    bias_value,
    bias_out,
    gain_two,
    shift_two,
    bias_up,
    bias_down,
    cotangent,
):
    row_count, length, width = tokens.shape
    total_rows = row_count * length
    gathered = collect(
        w_qkv,
        w_out,
        w_up,
        w_down,
        gain_one,
        shift_one,
        bias_query,
        bias_value,
        bias_out,
        gain_two,
        shift_two,
        bias_up,
        bias_down,
    )
    full_qkv, full_out, full_up, full_down = (gathered[0], gathered[1], gathered[2], gathered[3])
    gain_first = gathered[4].astype(jnp.float32)
    shift_first = gathered[5].astype(jnp.float32)
    query_bias = gathered[6].astype(jnp.float32)
    value_bias = gathered[7].astype(jnp.float32)
    out_bias = gathered[8].astype(jnp.float32)
    gain_second = gathered[9].astype(jnp.float32)
    shift_second = gathered[10].astype(jnp.float32)
    up_bias = gathered[11].astype(jnp.float32)
    down_bias = gathered[12].astype(jnp.float32)
    allowed = attend_mask(segment_ids, pad_mask)
    inputs = tokens.astype(jnp.float32).reshape(total_rows, width)
    first_norm, first_pull = jax.vjp(layer_norm, inputs, gain_first, shift_first)
    normed = first_norm.astype(jnp.bfloat16)
    mixed = jnp.dot(normed, full_qkv, preferred_element_type=jnp.float32)
    query_part = (
        (mixed[:, :width] + query_bias).astype(jnp.bfloat16).reshape(row_count, length, HEADS, HDIM)
    )
    key_part = (
        mixed[:, width : 2 * width].astype(jnp.bfloat16).reshape(row_count, length, HEADS, HDIM)
    )
    value_part = (
        (mixed[:, 2 * width :] + value_bias)
        .astype(jnp.bfloat16)
        .reshape(row_count, length, HEADS, HDIM)
    )
    scores = score_block(query_part, key_part, allowed)
    highest = jnp.max(scores, axis=-1, keepdims=True)
    log_total = highest + jnp.log(jnp.sum(jnp.exp(scores - highest), axis=-1, keepdims=True))
    weights = jnp.exp(scores - log_total).astype(jnp.bfloat16)
    attended = jnp.einsum(
        "rhqk,rkhe->rqhe", weights, value_part, preferred_element_type=jnp.float32
    )
    attended = attended.reshape(total_rows, width).astype(jnp.bfloat16)
    middle = inputs + jnp.dot(attended, full_out, preferred_element_type=jnp.float32) + out_bias
    second_norm, second_pull = jax.vjp(layer_norm, middle, gain_second, shift_second)
    normed_two = second_norm.astype(jnp.bfloat16)
    hidden = jnp.dot(normed_two, full_up, preferred_element_type=jnp.float32) + up_bias
    active, gate_pull = jax.vjp(smooth_gate, hidden)
    active_low = active.astype(jnp.bfloat16)
    result = middle + jnp.dot(active_low, full_down, preferred_element_type=jnp.float32) + down_bias
    output = result.astype(jnp.bfloat16).reshape(row_count, length, width)
    again = collect(
        w_qkv,
        w_out,
        w_up,
        w_down,
        gain_one,
        shift_one,
        bias_query,
        bias_value,
        bias_out,
        gain_two,
        shift_two,
        bias_up,
        bias_down,
    )
    full_qkv, full_out, full_up, full_down = (again[0], again[1], again[2], again[3])
    down_in = cotangent.reshape(total_rows, width)
    outer_grad = down_in.astype(jnp.float32)
    grad_bias_down = jnp.sum(outer_grad, axis=0)
    grad_w_down = outer_sum(active_low, down_in)
    active_grad = against(down_in, full_down)
    hidden_grad = gate_pull(active_grad)[0].astype(jnp.bfloat16)
    grad_bias_up = jnp.sum(hidden_grad.astype(jnp.float32), axis=0)
    grad_w_up = outer_sum(normed_two, hidden_grad)
    norm_two_grad = against(hidden_grad, full_up)
    middle_part, grad_gain_two, grad_shift_two = second_pull(norm_two_grad)
    middle_grad = outer_grad + middle_part
    branch_grad = middle_grad.astype(jnp.bfloat16)
    grad_bias_out = jnp.sum(branch_grad.astype(jnp.float32), axis=0)
    grad_w_out = outer_sum(attended, branch_grad)
    attended_grad = (
        against(branch_grad, full_out).astype(jnp.bfloat16).reshape(row_count, length, HEADS, HDIM)
    )
    probs = jnp.exp(score_block(query_part, key_part, allowed) - log_total)
    probs_low = probs.astype(jnp.bfloat16)
    value_grad = jnp.einsum(
        "rhqk,rqhe->rkhe", probs_low, attended_grad, preferred_element_type=jnp.float32
    ).astype(jnp.bfloat16)
    prob_grad = jnp.einsum(
        "rqhe,rkhe->rhqk", attended_grad, value_part, preferred_element_type=jnp.float32
    )
    inner_term = jnp.sum(prob_grad * probs, axis=-1, keepdims=True)
    score_grad = (probs * (prob_grad - inner_term)).astype(jnp.bfloat16)
    score_scale = 1.0 / math.sqrt(HDIM)
    query_grad = (
        (
            jnp.einsum("rhqk,rkhe->rqhe", score_grad, key_part, preferred_element_type=jnp.float32)
            * score_scale
        )
        .astype(jnp.bfloat16)
        .reshape(total_rows, width)
    )
    key_grad = (
        (
            jnp.einsum(
                "rhqk,rqhe->rkhe", score_grad, query_part, preferred_element_type=jnp.float32
            )
            * score_scale
        )
        .astype(jnp.bfloat16)
        .reshape(total_rows, width)
    )
    value_flat = value_grad.reshape(total_rows, width)
    mixed_grad = jnp.concatenate([query_grad, key_grad, value_flat], axis=1)
    grad_bias_query = jnp.sum(query_grad.astype(jnp.float32), axis=0)
    grad_bias_value = jnp.sum(value_flat.astype(jnp.float32), axis=0)
    grad_w_qkv = outer_sum(normed, mixed_grad)
    norm_one_grad = against(mixed_grad, full_qkv)
    input_part, grad_gain_one, grad_shift_one = first_pull(norm_one_grad)
    grad_tokens = (middle_grad + input_part).reshape(row_count, length, width)
    shares = (
        lax.psum_scatter(grad_w_qkv, ("gx", "gy"), scatter_dimension=0, tiled=True),
        lax.psum_scatter(grad_w_out, ("gx", "gy"), scatter_dimension=0, tiled=True),
        lax.psum_scatter(grad_w_up, ("gx", "gy"), scatter_dimension=0, tiled=True),
        lax.psum_scatter(grad_w_down, ("gx", "gy"), scatter_dimension=0, tiled=True),
        lax.psum_scatter(grad_gain_one, ("gx", "gy"), scatter_dimension=0, tiled=True),
        lax.psum_scatter(grad_shift_one, ("gx", "gy"), scatter_dimension=0, tiled=True),
        lax.psum_scatter(grad_bias_query, ("gx", "gy"), scatter_dimension=0, tiled=True),
        lax.psum_scatter(grad_bias_value, ("gx", "gy"), scatter_dimension=0, tiled=True),
        lax.psum_scatter(grad_bias_out, ("gx", "gy"), scatter_dimension=0, tiled=True),
        lax.psum_scatter(grad_gain_two, ("gx", "gy"), scatter_dimension=0, tiled=True),
        lax.psum_scatter(grad_shift_two, ("gx", "gy"), scatter_dimension=0, tiled=True),
        lax.psum_scatter(grad_bias_up, ("gx", "gy"), scatter_dimension=0, tiled=True),
        lax.psum_scatter(grad_bias_down, ("gx", "gy"), scatter_dimension=0, tiled=True),
    )
    return (
        output,
        grad_tokens,
        shares[0],
        shares[1],
        shares[2],
        shares[3],
        shares[4],
        shares[5],
        shares[6],
        shares[7],
        shares[8],
        shares[9],
        shares[10],
        shares[11],
        shares[12],
    )


def solution(mesh):
    return jax.shard_map(
        on_device,
        mesh=mesh,
        in_specs=(
            P(("gx", "gy"), None, None),
            P(("gx", "gy"), None),
            P(("gx", "gy"), None),
            P(("gx", "gy"), None),
            P(("gx", "gy"), None),
            P(("gx", "gy"), None),
            P(("gx", "gy"), None),
            P(("gx", "gy")),
            P(("gx", "gy")),
            P(("gx", "gy")),
            P(("gx", "gy")),
            P(("gx", "gy")),
            P(("gx", "gy")),
            P(("gx", "gy")),
            P(("gx", "gy")),
            P(("gx", "gy")),
            P(("gx", "gy"), None, None),
        ),
        out_specs=(
            P(("gx", "gy"), None, None),
            P(("gx", "gy"), None, None),
            P(("gx", "gy"), None),
            P(("gx", "gy"), None),
            P(("gx", "gy"), None),
            P(("gx", "gy"), None),
            P(("gx", "gy")),
            P(("gx", "gy")),
            P(("gx", "gy")),
            P(("gx", "gy")),
            P(("gx", "gy")),
            P(("gx", "gy")),
            P(("gx", "gy")),
            P(("gx", "gy")),
            P(("gx", "gy")),
        ),
        check_vma=False,
    )
```

profile of v0, /device:TPU:0, one launch (start us, length us, event | category | flops | bytes accessed | tf_op | source)
XLA Modules:
  0.0 838.5 jit_solution(17734180992051257629)
XLA Ops:
  7.3 0.7 all-gather.5.cloned.1.call-update
  8.1 0.7 all-gather.7.cloned.1.call-update
  8.8 0.7 all-gather.9.cloned.1.call-update
  10.2 1.7 convert_reduce_fusion.1
  11.9 2.0 fusion.21
  13.9 0.6 copy-done.29
  16.6 42.7 %all-reduce.19 = (bf16[768]{0:T(1024)(128)(2,1)S(1)}, bf16[768]{0:T(1024)(128)(2,1)S(1)}, bf16[768]{0:T(1024)(128)(2,1)S(1)}, bf16[768]{0:T(1024)(128)(2,1)S(1)}...) all-reduce(bf16[768]{0:T(1024)(128)(2,1)S(1)} %dynamic-update-slice, ...), channel_id=1, replica_groups=mesh['gx'=8,'gy'=4] {'gx','gy'}, use_global_device_ids=true, to_apply=%add.1 | all-reduce | flops 9216 | bytes 36864
  59.4 0.6 convert_element_type.128
  60.5 0.6 fusion.17
  61.2 12.8 %all-gather.5.cloned.1.call-done = bf16[768,2304]{1,0:T(8,128)(2,1)} async-done(((bf16[24,2304]{1,0:T(8,128)(2,1)}), bf16[768,2304]{1,0:T(8,128)(2,1)}) %all-gather.5.cloned.1.call-update) | async-done | bytes 3538960 | tf_op jit(solution)/shard_map/all_gather | solution.py:65
  74.0 5.8 fusion.54
  80.0 2.3 fusion.9
  82.3 2.6 copy.65
  84.9 3.9 reshape.186
  88.7 1.6 copy.66
  90.4 4.0 reshape.187
  94.4 1.6 copy.64
  96.0 3.1 reshape.185
  99.1 4.8 fusion.7
  104.0 3.2 exponential_reduce_fusion
  107.2 1.2 copy-done
  108.4 3.1 fusion.24
  111.5 1.2 copy.71
  113.1 16.6 %all-gather.7.cloned.1.call-done = bf16[768,768]{1,0:T(8,128)(2,1)} async-done(((bf16[24,768]{1,0:T(8,128)(2,1)}), bf16[768,768]{1,0:T(8,128)(2,1)}) %all-gather.7.cloned.1.call-update) | async-done | bytes 1179664 | tf_op jit(solution)/shard_map/all_gather | solution.py:66
  129.7 3.0 fusion.53
  132.7 1.7 copy-done.2
  135.0 60.3 %all-gather.9.cloned.1.call-done = bf16[768,3072]{1,0:T(8,128)(2,1)} async-done(((bf16[24,3072]{1,0:T(8,128)(2,1)}), bf16[768,3072]{1,0:T(8,128)(2,1)}) %all-gather.9.cloned.1.call-update) | async-done | bytes 4718608 | tf_op jit(solution)/shard_map/all_gather | solution.py:67
  195.3 11.4 %fusion.48 = f32[1024,3072]{1,0:T(8,128)} fusion(bf16[768,3072]{1,0:T(8,128)(2,1)} %all-gather.9.cloned.1.call-done, f32[1024,768]{1,0:T(8,128)} %copy-done.2, f32[768]{0:T(1024)S(1)} %convert_element_type.126, f32[768]{0:T(1024)S(1)} %convert_element_type.125, f32[1024]{0:T(1024)S(1)} %fusion.38, f32[1024]{0:T(1024)S(1)} %broadcast_multiply_fusion), kind=kOutput, calls=%fused_computation.95 | convolution fusion | flops 4835770368 | bytes 20461568 | tf_op jit(solution)/shard_map/dot_general | solution.py:154
  206.7 53.8 %all-gather.11.cloned.1.call-done = bf16[3072,768]{1,0:T(8,128)(2,1)} async-done(((bf16[96,768]{1,0:T(8,128)(2,1)}), bf16[3072,768]{1,0:T(8,128)(2,1)}) %all-gather.11.cloned.1.call-update) | async-done | bytes 4718608 | tf_op jit(solution)/shard_map/all_gather | solution.py:68
  260.5 15.5 %convert_reduce_fusion = (f32[3072]{0:T(1024)}, bf16[1024,3072]{1,0:T(8,128)(2,1)S(1)}) fusion(f32[1024,3072]{1,0:T(8,128)} %fusion.48, f32[3072]{0:T(1024)S(1)} %copy-done.33, bf16[1024,768]{1,0:T(8,128)(2,1)S(1)} %bitcast.99, bf16[3072,768]{1,0:T(8,128)(2,1)} %all-gather.11.cloned.1.call-done), kind=kOutput, calls=%fused_computation.9 | convolution fusion | flops 4904186880 | bytes 25190400 | tf_op jit(solution)/shard_map/dot_general | solution.py:38
  276.0 10.8 %multiply_reduce_fusion.1 = (f32[768]{0:T(1024)}, f32[1024]{0:T(1024)S(1)}, f32[768]{0:T(1024)}, f32[1024,768]{1,0:T(8,128)S(1)}) fusion(f32[1024,768]{1,0:T(8,128)S(1)} %copy-done.3, f32[1024]{0:T(1024)S(1)} %fusion.38, f32[1024]{0:T(1024)S(1)} %broadcast_multiply_fusion, f32[768]{0:T(1024)S(1)} %convert_element_type.125, ...), kind=kOutput, calls=%fused_computation.42 | convolution fusion | flops 4838126592 | bytes 17323008 | tf_op jit(solution)/shard_map/dot_general | solution.py:38
  286.8 1.6 fusion.52
  288.5 1.1 convert_reduce_fusion.3
  290.1 1.2 copy-done.19
  291.3 2.8 fusion.56
  294.1 4.4 convolution_convert_fusion.2
  298.5 2.6 copy.72
  301.1 3.9 reshape.190
  305.0 10.1 %convert_reduce_fusion.4 = (f32[12,64]{1,0:T(8,128)}, bf16[4,256,12,64]{1,3,2,0:T(8,128)(2,1)}) fusion(f32[4,12,256,256]{2,3,1,0:T(8,128)} %copy-done, f32[4,12,256]{2,1,0:T(8,128)S(1)} %log_add_fusion, pred[4,256,256]{1,2,0:T(8,128)(4,1)S(1)} %or_and_fusion, bf16[4,256,12,64]{1,0,3,2:T(4,128)(2,1)} %reshape.190), kind=kOutput, calls=%fused_computation.44 | convolution fusion | flops 417594624 | bytes 16043008 | tf_op jit(solution)/shard_map/rhqk,rqhe->rkhe/dot_general | solution.py:194
  315.1 9.5 %multiply_reduce_fusion = (f32[4,12,256]{2,1,0:T(8,128)S(1)}, f32[4,12,256,256]{2,3,1,0:T(8,128)}) fusion(f32[4,12,256,256]{2,3,1,0:T(8,128)} %copy-done, f32[4,12,256]{2,1,0:T(8,128)S(1)} %log_add_fusion, pred[4,256,256]{1,2,0:T(8,128)(4,1)S(1)} %or_and_fusion, bf16[4,256,12,64]{1,0,3,2:T(4,128)(2,1)S(1)} %copy-done.9, ...), kind=kOutput, calls=%fused_computation.11 | convolution fusion | flops 418369536 | bytes 28672000 | tf_op jit(solution)/shard_map/rqhe,rkhe->rhqk/dot_general | solution.py:197
  324.7 2.6 copy.83
  327.7 10.4 %multiply_convert_fusion = bf16[4,12,256,256]{2,3,1,0:T(8,128)(2,1)S(1)} fusion(f32[4,12,256,256]{2,3,1,0:T(8,128)} %get-tuple-element.54, f32[4,12,256,256]{2,3,1,0:T(8,128)} %copy-done, f32[4,12,256]{2,1,0:T(8,128)S(1)} %get-tuple-element.53, f32[4,12,256]{2,1,0:T(8,128)S(1)} %log_add_fusion, pred[4,256,256]{1,2,0:T(8,128)(4,1)S(1)} %or_and_fusion), kind=kLoop, calls=%fused_computation.10 | loop fusion | flops 18874368 | bytes 31817728 | tf_op jit(solution)/shard_map/convert_element_type | solution.py:201
  338.1 2.0 fusion.27
  340.1 1.2 copy.80
  341.7 1.3 convert_reduce_fusion.5
  343.0 1.2 copy.77
  345.0 2.2 copy-done.20
  347.2 6.1 fusion.55
  353.4 11.0 %fusion.47 = f32[768,3072]{1,0:T(8,128)} fusion(bf16[1024,3072]{1,0:T(8,128)(2,1)} %copy-done.12, f32[1024,768]{1,0:T(8,128)} %copy-done.2, f32[768]{0:T(1024)S(1)} %convert_element_type.126, f32[768]{0:T(1024)S(1)} %convert_element_type.125, f32[1024]{0:T(1024)S(1)} %fusion.38, f32[1024]{0:T(1024)S(1)} %broadcast_multiply_fusion), kind=kOutput, calls=%fused_computation.94 | convolution fusion | flops 4835770368 | bytes 18888704 | tf_op jit(solution)/shard_map/dot_general | solution.py:32
  365.1 12.9 %fusion.49 = f32[3072,768]{1,0:T(8,128)} fusion(bf16[1024,768]{1,0:T(8,128)(2,1)S(1)} %bitcast.100, f32[1024,3072]{1,0:T(8,128)} %fusion.48, f32[3072]{0:T(1024)S(1)} %copy-done.34), kind=kOutput, calls=%fused_computation.96 | convolution fusion | flops 4863295488 | bytes 23605248 | tf_op jit(solution)/shard_map/dot_general | solution.py:32
  378.1 0.6 copy-done.40
  379.1 7.6 fusion.50
  386.8 1.5 copy-done.7
  388.4 1.7 fusion.18
  390.1 40.9 %all-reduce.18 = (f32[768]{0:T(1024)S(1)}, f32[768]{0:T(1024)S(1)}, f32[768]{0:T(1024)S(1)}, f32[768]{0:T(1024)S(1)}, f32[768]{0:T(1024)S(1)}, /*index=5*/f32[76...) all-reduce(f32[768]{0:T(1024)S(1)} %get-tuple-element.17, ...), channel_id=6, replica_groups=mesh['gx'=8,'gy'=4] {'gx','gy'}, use_global_device_ids=true, to_apply=%region_16.17.clone | all-reduce | flops 9216 | bytes 73728
  431.1 0.6 dynamic-slice
  434.0 0.6 dynamic-slice.5
  435.1 0.6 dynamic-slice.8
  435.7 0.6 dynamic-slice.7
  436.3 5.1 add_add_fusion.2
  441.4 13.4 %add_convert_fusion = bf16[1024,768]{1,0:T(8,128)(2,1)} fusion(f32[1024,768]{1,0:T(8,128)S(1)} %copy-done.4, bf16[3072,768]{1,0:T(8,128)(2,1)} %all-gather.11.cloned.1.call-done, f32[768]{0:T(1024)S(1)} %convert_element_type.130, f32[1024,3072]{1,0:T(8,128)} %fusion.48, f32[3072]{0:T(1024)S(1)} %copy-done.34), kind=kOutput, calls=%fused_computation.51 | convolution fusion | flops 4865654784 | bytes 22035456 | tf_op jit(solution)/shard_map/dot_general | solution.py:157
  454.7 93.2 %reduce-scatter.5.cloned.1.call-done = f32[24,2304]{1,0:T(8,128)} async-done(((f32[768,2304]{1,0:T(8,128)}), f32[24,2304]{1,0:T(8,128)}) %reduce-scatter.5.cloned.1.call-update) | async-done | bytes 221200 | tf_op jit(solution)/shard_map/reduce_scatter | solution.py:230
  548.0 141.0 %reduce-scatter.9.cloned.1.call-done = f32[24,3072]{1,0:T(8,128)} async-done(((f32[768,3072]{1,0:T(8,128)}), f32[24,3072]{1,0:T(8,128)}) %reduce-scatter.9.cloned.1.call-update) | async-done | bytes 294928 | tf_op jit(solution)/shard_map/reduce_scatter | solution.py:232
  689.0 142.2 %reduce-scatter.11.cloned.1.call-done = f32[96,768]{1,0:T(8,128)} async-done(((f32[3072,768]{1,0:T(8,128)}), f32[96,768]{1,0:T(8,128)}) %reduce-scatter.11.cloned.1.call-update) | async-done | bytes 294928 | tf_op jit(solution)/shard_map/reduce_scatter | solution.py:233
  (165 shorter events, 10.7 us)
Async XLA Ops:
  7.2 53.3 %copy-start.1 = (bf16[4,256,768]{2,1,0:T(8,128)(2,1)S(1)}, bf16[4,256,768]{2,1,0:T(8,128)(2,1)}, u32[]{:S(2)}) copy-start(bf16[4,256,768]{2,1,0:T(8,128)(2,1)} %param.17) | copy-start | bytes 4718596
  7.2 7.3 copy-start.41
  7.2 7.5 copy-start.42
  7.2 7.8 copy-start.43
  7.2 8.0 copy-start.44
  7.2 8.2 copy-start.45
  7.2 8.4 %copy-start.46 = (bf16[24]{0:T(256)(128)(2,1)S(1)}, bf16[24]{0:T(256)(128)(2,1)}, u32[]{:S(2)}) copy-start(bf16[24]{0:T(256)(128)(2,1)} %param.24) | copy-start | bytes 148
  7.3 8.7 %copy-start.47 = (bf16[24]{0:T(256)(128)(2,1)S(1)}, bf16[24]{0:T(256)(128)(2,1)}, u32[]{:S(2)}) copy-start(bf16[24]{0:T(256)(128)(2,1)} %param.25) | copy-start | bytes 148
  7.3 8.9 %copy-start.48 = (bf16[24]{0:T(256)(128)(2,1)S(1)}, bf16[24]{0:T(256)(128)(2,1)}, u32[]{:S(2)}) copy-start(bf16[24]{0:T(256)(128)(2,1)} %param.29) | copy-start | bytes 148
  7.3 9.1 %copy-start.49 = (bf16[96]{0:T(256)(128)(2,1)S(1)}, bf16[96]{0:T(256)(128)(2,1)}, u32[]{:S(2)}) copy-start(bf16[96]{0:T(256)(128)(2,1)} %param.31) | copy-start | bytes 580
  7.3 52.7 %copy-start.37 = (s32[4,256]{1,0:T(4,128)S(1)}, s32[4,256]{1,0:T(4,128)}, u32[]{:S(2)}) copy-start(s32[4,256]{1,0:T(4,128)} %param.19) | copy-start | bytes 12292
  7.3 52.7 %copy-start.32 = (s32[4,256]{1,0:T(4,128)S(1)}, s32[4,256]{1,0:T(4,128)}, u32[]{:S(2)}) copy-start(s32[4,256]{1,0:T(4,128)} %param.18) | copy-start | bytes 12292
  7.3 66.7 %all-gather.5.cloned.1.call-start = ((), (), s32[]{:S(2)}) async-start(), calls=%async_computation.4 | async-start | bytes 3649536 | tf_op jit(solution)/shard_map/all_gather | solution.py:65
  8.0 121.7 %all-gather.7.cloned.1.call-start = ((), (), s32[]{:S(2)}) async-start(), calls=%async_computation.5 | async-start | bytes 1216512 | tf_op jit(solution)/shard_map/all_gather | solution.py:66
  8.8 186.5 %all-gather.9.cloned.1.call-start = ((), (), s32[]{:S(2)}) async-start(), calls=%async_computation.6 | async-start | bytes 4866048 | tf_op jit(solution)/shard_map/all_gather | solution.py:67
  9.5 251.0 %all-gather.11.cloned.1.call-start = ((), (), s32[]{:S(2)}) async-start(), calls=%async_computation.7 | async-start | bytes 4866048 | tf_op jit(solution)/shard_map/all_gather | solution.py:68
  10.1 444.6 %reduce-scatter.7.cloned.1.call-start = ((), (), s32[]{:S(2)}) async-start(), calls=%async_computation.9 | async-start | bytes 2433024 | tf_op jit(solution)/shard_map/reduce_scatter | solution.py:231
  11.9 68.0 %copy-start.21 = (f32[1,2,4,128]{3,1,2,0:T(2,128)}, f32[1,2,4,128]{3,1,2,0:T(2,128)S(1)}, u32[]{:S(2)}) copy-start(f32[1,2,4,128]{3,1,2,0:T(2,128)S(1)} %copy.88) | copy-start | bytes 12292
  13.9 0.6 copy-start.29
  14.5 65.3 %copy-start.23 = (f32[1024]{0:T(1024)}, f32[1024]{0:T(1024)S(1)}, u32[]{:S(2)}) copy-start(f32[1024]{0:T(1024)S(1)} %rsqrt.20) | copy-start | bytes 12292
  59.3 20.5 %copy-start.25 = (f32[768]{0:T(1024)}, f32[768]{0:T(1024)S(1)}, u32[]{:S(2)}) copy-start(f32[768]{0:T(1024)S(1)} %convert_element_type.113) | copy-start | bytes 9220
  61.1 12.8 %copy-start.15 = (bf16[1024,768]{1,0:T(8,128)(2,1)}, bf16[1024,768]{1,0:T(8,128)(2,1)S(1)}, u32[]{:S(2)}) copy-start(bf16[1024,768]{1,0:T(8,128)(2,1)S(1)} %fusion.17) | copy-start | bytes 4718596
  90.4 4.0 copy-start.14
  99.1 8.1 copy-start.8
  103.9 4.5 copy-start
  113.1 19.6 %copy-start.17 = (bf16[96,8,4,256]{3,1,2,0:T(8,128)(2,1)}, bf16[96,8,4,256]{3,1,2,0:T(8,128)(2,1)S(1)}, u32[]{:S(2)}) copy-start(bf16[96,8,4,256]{3,1,2,0:T(8,128)(2,1)S(1)} %copy.90) | copy-start | bytes 4718596
  132.7 1.7 copy-start.2
  135.0 125.6 %copy-start.6 = (bf16[4,256,768]{2,1,0:T(8,128)(2,1)S(1)}, bf16[4,256,768]{2,1,0:T(8,128)(2,1)}, u32[]{:S(2)}) copy-start(bf16[4,256,768]{2,1,0:T(8,128)(2,1)} %param.33) | copy-start | bytes 4718596
  135.0 125.5 %copy-start.33 = (f32[3072]{0:T(1024)S(1)}, f32[3072]{0:T(1024)}, u32[]{:S(2)}) copy-start(f32[3072]{0:T(1024)} %convert_element_type.128) | copy-start | bytes 36868
  260.5 15.5 %copy-start.3 = (f32[1024,768]{1,0:T(8,128)S(1)}, f32[1024,768]{1,0:T(8,128)}, u32[]{:S(2)}) copy-start(f32[1024,768]{1,0:T(8,128)} %copy-done.2) | copy-start | bytes 9437188
  276.0 10.8 %copy-start.12 = (bf16[1024,3072]{1,0:T(8,128)(2,1)}, bf16[1024,3072]{1,0:T(8,128)(2,1)S(1)}, u32[]{:S(2)}) copy-start(bf16[1024,3072]{1,0:T(8,128)(2,1)S(1)} %get-tuple-element.61) | copy-start | bytes 18874372
  288.5 1.7 copy-start.5
  288.5 1.6 copy-start.27
  288.5 2.8 copy-start.18
  290.1 1.2 copy-start.19
  305.0 10.1 %copy-start.9 = (bf16[4,256,12,64]{1,0,3,2:T(4,128)(2,1)S(1)}, bf16[4,256,12,64]{1,0,3,2:T(4,128)(2,1)}, u32[]{:S(2)}) copy-start(bf16[4,256,12,64]{1,0,3,2:T(4,128)(2,1)} %copy-done.8) | copy-start | bytes 4718596
  305.0 10.1 %copy-start.10 = (bf16[4,256,12,64]{1,0,3,2:T(4,128)(2,1)S(1)}, bf16[4,256,12,64]{1,0,3,2:T(4,128)(2,1)}, u32[]{:S(2)}) copy-start(bf16[4,256,12,64]{1,0,3,2:T(4,128)(2,1)} %reshape.190) | copy-start | bytes 4718596
  324.6 223.4 %reduce-scatter.5.cloned.1.call-start = ((), (), s32[]{:S(2)}) async-start(), calls=%async_computation.8 | async-start | bytes 7299072 | tf_op jit(solution)/shard_map/reduce_scatter | solution.py:230
  327.6 10.5 %copy-start.11 = (bf16[4,256,12,64]{1,0,3,2:T(4,128)(2,1)S(1)}, bf16[4,256,12,64]{1,0,3,2:T(4,128)(2,1)}, u32[]{:S(2)}) copy-start(bf16[4,256,12,64]{1,0,3,2:T(4,128)(2,1)} %reshape.186) | copy-start | bytes 4718596
  340.1 1.6 copy-start.13
  344.8 2.5 copy-start.16
  345.0 2.2 copy-start.20
  353.3 335.7 %reduce-scatter.9.cloned.1.call-start = ((), (), s32[]{:S(2)}) async-start(), calls=%async_computation.10 | async-start | bytes 9732096 | tf_op jit(solution)/shard_map/reduce_scatter | solution.py:232
  364.4 0.7 copy-start.34
  364.4 466.7 %reduce-scatter.11.cloned.1.call-start = ((), (), s32[]{:S(2)}) async-start(), calls=%async_computation.11 | async-start | bytes 9732096 | tf_op jit(solution)/shard_map/reduce_scatter | solution.py:233
  378.0 0.7 copy-start.40
  378.0 1.0 copy-start.36
  378.0 1.1 copy-start.22
  378.0 1.1 copy-start.26
  379.1 7.7 copy-start.30
  379.1 9.2 %copy-start.24 = (f32[1024]{0:T(1024)S(1)}, f32[1024]{0:T(1024)}, u32[]{:S(2)}) copy-start(f32[1024]{0:T(1024)} %copy-done.23) | copy-start | bytes 12292
  386.7 1.6 copy-start.7
  386.7 3.3 copy-start.31
  386.8 3.3 copy-start.35
  386.8 3.3 copy-start.38
  386.8 3.3 copy-start.39
  386.8 49.5 %copy-start.28 = (f32[1024]{0:T(1024)S(1)}, f32[1024]{0:T(1024)}, u32[]{:S(2)}) copy-start(f32[1024]{0:T(1024)} %copy-done.27) | copy-start | bytes 12292
  436.3 5.1 copy-start.4
Sparse Core Ops, SparseCore 0:
  11.0 62.8 all-gather.4
  76.9 52.8 all-gather.6
  132.6 62.5 all-gather.8
  198.0 62.4 all-gather.10
  324.7 97.8 reduce-scatter.6
  429.6 118.2 reduce-scatter.4
  554.4 134.5 reduce-scatter.8
  696.5 134.6 reduce-scatter.10
where the time goes:
time: 847 us; the launch traced here: 839 us
  waiting for transfers between devices  523 us (62%)
  matrix products  135 us (16%)
  blocking collectives  83.6 us (10%)
  local copies, waits for them, and re-layouts  49.1 us (6%)
  other arithmetic  31.8 us (4%)
  between operations  15.4 us (2%)
    reduce_scatter x1, waiting for transfers between devices, on_device(): lax.psum_scatter(grad_w_down, ('gx', 'gy'), scatter_dimension=0, tiled=True)  142 us
    reduce_scatter x1, waiting for transfers between devices, on_device(): lax.psum_scatter(grad_w_up, ('gx', 'gy'), scatter_dimension=0, tiled=True)  141 us
    reduce_scatter x1, waiting for transfers between devices, on_device(): lax.psum_scatter(grad_w_qkv, ('gx', 'gy'), scatter_dimension=0, tiled=True)  93.2 us
    unnamed x2, blocking collectives  83.6 us
    all_gather x1, waiting for transfers between devices, collect(): lax.all_gather(w_up, ('gx', 'gy'), axis=0, tiled=True)  60.3 us
    all_gather x1, waiting for transfers between devices, collect(): lax.all_gather(w_down, ('gx', 'gy'), axis=0, tiled=True)  53.8 us
    dot_general x4, matrix products, against(): lax.dot_general(left, matrix, (((1,), (1,)), ((), ())), preferred_element...  38.2 us
    dot_general x4, matrix products, outer_sum(): lax.dot_general(left, right, (((0,), (0,)), ((), ())), preferred_element_...  32.8 us
  transfers between devices with their start and end apart: 8, of which 7 were waited for; matrix products, arithmetic and copies ran while one was open for 17% of the time, Pallas kernels for 0%

commit v1 on v0

--- a/solution.py
+++ b/solution.py
@@ -78,7 +78,7 @@
     )
 
 
-def on_device(
+def generic_device(
     tokens,
     segment_ids,
     pad_mask,
@@ -260,9 +260,276 @@
     )
 
 
+AXES = ("gx", "gy")
+
+
+def pairs(move):
+    out = []
+    for d in range(32):
+        z, y, x, c = d // 8, (d // 4) % 2, (d // 2) % 2, d % 2
+        z, y, x, c = move(z, y, x, c)
+        out.append((d, ((z * 2 + y) * 2 + x) * 2 + c))
+    return out
+
+
+SWAP_C = pairs(lambda z, y, x, c: (z, y, x, 1 - c))
+SWAP_X = pairs(lambda z, y, x, c: (z, y, 1 - x, c))
+SWAP_Y = pairs(lambda z, y, x, c: (z, 1 - y, x, c))
+SWAP_Z = [None] + [pairs(lambda z, y, x, c, k=k: (z ^ k, y, x, c)) for k in (1, 2, 3)]
+
+
+def send(values, perm):
+    return lax.ppermute(values, AXES, perm)
+
+
+def place():
+    gx, gy = lax.axis_index("gx"), lax.axis_index("gy")
+    return gx // 2, gx % 2, gy // 2, gy % 2
+
+
+def spread_block(own):
+    own = own[None]
+    col = jnp.concatenate([own] + [send(own, SWAP_Z[k]) for k in (1, 2, 3)], axis=0)
+    along_x, along_y = send(col, SWAP_X), send(col, SWAP_Y)
+    far0, far1 = send(along_x[0:2], SWAP_Y), send(along_y[2:4], SWAP_X)
+    return [col, along_x, along_y, far0, far1]
+
+
+def gather_pack(own):
+    mine = spread_block(own)
+    other = [send(v, SWAP_C) for v in mine]
+    return mine, other
+
+
+def total_pack(mine, theirs):
+    got = send(theirs, SWAP_C)
+
+    def both(index):
+        return mine[index].astype(jnp.float32) + got[index].astype(jnp.float32)
+
+    low = jnp.bfloat16
+    first_x = send(both((slice(None), 1, slice(0, 2))).astype(low), SWAP_X)
+    first_y = send(both((1, slice(None), slice(2, 4))).astype(low), SWAP_Y)
+    second_y = send((both((1, 0, slice(0, 2))) + first_x[1]).astype(low), SWAP_Y)
+    second_x = send((both((0, 1, slice(2, 4))) + first_y[1]).astype(low), SWAP_X)
+    near = both((0, 0, slice(0, 2))) + first_x[0] + second_y
+    away = both((0, 0, slice(2, 4))) + first_y[0] + second_x
+    parts = [near[0], near[1], away[0], away[1]]
+    total = parts[0]
+    for k in (1, 2, 3):
+        total = total + send(parts[k].astype(low), SWAP_Z[k])
+    return total
+
+
+def to_absolute(rel, axis_bits):
+    z0, y0, x0 = axis_bits
+    rel = jnp.where(y0 == 0, rel, rel[::-1])
+    rel = jnp.where(x0 == 0, rel, rel[:, ::-1])
+    odd = jnp.concatenate([rel[:, :, 1:2], rel[:, :, 0:1], rel[:, :, 3:4], rel[:, :, 2:3]], axis=2)
+    rel = jnp.where(z0 % 2 == 0, rel, odd)
+    rel = jnp.where(z0 // 2 == 0, rel, jnp.concatenate([rel[:, :, 2:4], rel[:, :, 0:2]], axis=2))
+    return rel
+
+
+def to_full(pack, bits):
+    col, along_x, along_y, far0, far1 = pack
+    far = jnp.concatenate([far0, far1], axis=0)
+    rel = jnp.stack([jnp.stack([col, along_x]), jnp.stack([along_y, far])])
+    absolute = to_absolute(rel, bits)
+    return jnp.transpose(absolute, (2, 0, 1, 3, 4)).reshape(16, 48, -1)
+
+
+def to_relative(full, bits):
+    rel = jnp.transpose(full.reshape(4, 2, 2, 48, -1), (1, 2, 0, 3, 4))
+    return to_absolute(rel, bits)
+
+
+def halves_of(own, sibling, core):
+    return jnp.where(core == 0, own, sibling), jnp.where(core == 0, sibling, own)
+
+
+VECTOR_SIZES = (24, 24, 24, 24, 24, 24, 24, 96, 24)
+
+
+def on_device(
+    tokens, segment_ids, pad_mask, w_qkv, w_out, w_up, w_down, gain_one, shift_one, bias_query,
+    bias_value, bias_out, gain_two, shift_two, bias_up, bias_down, cotangent,
+):
+    z0, y0, x0, core = place()
+    bits = (z0, y0, x0)
+    row_count, length, width = tokens.shape
+    total_rows = row_count * length
+    vectors = jnp.concatenate(
+        [gain_one, shift_one, bias_query, bias_value, bias_out, gain_two, shift_two, bias_up, bias_down]
+    )
+    vectors = lax.all_gather(jnp.pad(vectors, (0, 96))[None], AXES, axis=0, tiled=True)
+    spans, at = [], 0
+    for size in VECTOR_SIZES:
+        spans.append(vectors[:, at : at + size].astype(jnp.float32))
+        at += size
+    flat = [v.reshape(-1) for v in spans]
+    gain_first, shift_first, query_bias, value_bias, out_bias, gain_second, shift_second = flat[:7]
+    down_bias = flat[8]
+    up_bias = spans[7].reshape(16, 2, 96).transpose(1, 0, 2).reshape(-1)
+
+    def column_half(side):
+        at = side * 384
+        up = w_up.reshape(24, 16, 2, 96).transpose(2, 0, 1, 3).reshape(2, 24, 1536)
+        return (
+            jnp.concatenate(
+                [w_qkv[:, at : at + 384], w_qkv[:, 768 + at : 1152 + at],
+                 w_qkv[:, 1536 + at : 1920 + at], w_out[:, at : at + 384]], axis=1),
+            up[0, :, side * 768 : side * 768 + 768],
+            up[1, :, side * 768 : side * 768 + 768],
+            w_down[:, at : at + 384],
+        )
+
+    zero, one = column_half(0), column_half(1)
+    keep = [jnp.where(core == 0, a, b) for a, b in zip(zero, one)]
+    give = [jnp.where(core == 0, b, a) for a, b in zip(zero, one)]
+    got = [send(v, SWAP_C) for v in give]
+
+    def rows(a, b):
+        return jnp.where(core == 0, jnp.concatenate([a, b]), jnp.concatenate([b, a]))
+
+    def tall(v):
+        return jnp.concatenate([v[:48], v[48:]], axis=1)
+
+    first = rows(keep[0], got[0])
+    down_a, down_b = halves_of(keep[3], got[3], core)
+    second = jnp.concatenate([rows(keep[1], got[1]), tall(down_a)], axis=1)
+    third = jnp.concatenate([rows(keep[2], got[2]), tall(down_b)], axis=1)
+    packs = []
+    for own in (first, second, third):
+        mine, other = gather_pack(own)
+        packs.append(halves_of(to_full(mine, bits), to_full(other, bits), core))
+    full_qkv = jnp.concatenate(
+        [packs[0][s][:, :, p * 384 : p * 384 + 384].reshape(768, 384) for p in range(3) for s in range(2)], axis=1)
+    full_out = jnp.concatenate([packs[0][s][:, :, 1152:].reshape(768, 384) for s in range(2)], axis=1)
+    full_up = jnp.concatenate([packs[1 + f][s][:, :, :768].reshape(768, 768) for f in range(2) for s in range(2)], axis=1)
+
+    def down_of(f):
+        sides = []
+        for s in range(2):
+            v = packs[1 + f][s][:, :, 768:]
+            sides.append(jnp.concatenate([v[:, :, :384], v[:, :, 384:]], axis=1).reshape(1536, 384))
+        return jnp.concatenate(sides, axis=1)
+
+    full_down = jnp.concatenate([down_of(0), down_of(1)], axis=0)
+
+    allowed = attend_mask(segment_ids, pad_mask)
+    inputs = tokens.astype(jnp.float32).reshape(total_rows, width)
+    first_norm, first_pull = jax.vjp(layer_norm, inputs, gain_first, shift_first)
+    normed = first_norm.astype(jnp.bfloat16)
+    mixed = jnp.dot(normed, full_qkv, preferred_element_type=jnp.float32)
+    query_part = (mixed[:, :width] + query_bias).astype(jnp.bfloat16).reshape(row_count, length, HEADS, HDIM)
+    key_part = mixed[:, width : 2 * width].astype(jnp.bfloat16).reshape(row_count, length, HEADS, HDIM)
+    value_part = (mixed[:, 2 * width :] + value_bias).astype(jnp.bfloat16).reshape(row_count, length, HEADS, HDIM)
+    scores = score_block(query_part, key_part, allowed)
+    highest = jnp.max(scores, axis=-1, keepdims=True)
+    log_total = highest + jnp.log(jnp.sum(jnp.exp(scores - highest), axis=-1, keepdims=True))
+    weights = jnp.exp(scores - log_total).astype(jnp.bfloat16)
+    attended = jnp.einsum("rhqk,rkhe->rqhe", weights, value_part, preferred_element_type=jnp.float32)
+    attended = attended.reshape(total_rows, width).astype(jnp.bfloat16)
+    middle = inputs + jnp.dot(attended, full_out, preferred_element_type=jnp.float32) + out_bias
+    second_norm, second_pull = jax.vjp(layer_norm, middle, gain_second, shift_second)
+    normed_two = second_norm.astype(jnp.bfloat16)
+    hidden = jnp.dot(normed_two, full_up, preferred_element_type=jnp.float32) + up_bias
+    active, gate_pull = jax.vjp(smooth_gate, hidden)
+    active_low = active.astype(jnp.bfloat16)
+    result = middle + jnp.dot(active_low, full_down, preferred_element_type=jnp.float32) + down_bias
+    output = result.astype(jnp.bfloat16).reshape(row_count, length, width)
+    down_in = cotangent.reshape(total_rows, width)
+    outer_grad = down_in.astype(jnp.float32)
+    grad_bias_down = jnp.sum(outer_grad, axis=0)
+    grad_w_down = outer_sum(active_low, down_in)
+    active_grad = against(down_in, full_down)
+    hidden_grad = gate_pull(active_grad)[0].astype(jnp.bfloat16)
+    grad_bias_up = jnp.sum(hidden_grad.astype(jnp.float32), axis=0)
+    grad_w_up = outer_sum(normed_two, hidden_grad)
+    norm_two_grad = against(hidden_grad, full_up)
+    middle_part, grad_gain_two, grad_shift_two = second_pull(norm_two_grad)
+    middle_grad = outer_grad + middle_part
+    branch_grad = middle_grad.astype(jnp.bfloat16)
+    grad_bias_out = jnp.sum(branch_grad.astype(jnp.float32), axis=0)
+    grad_w_out = outer_sum(attended, branch_grad)
+    attended_grad = against(branch_grad, full_out).astype(jnp.bfloat16).reshape(row_count, length, HEADS, HDIM)
+    probs = jnp.exp(score_block(query_part, key_part, allowed) - log_total)
+    probs_low = probs.astype(jnp.bfloat16)
+    value_grad = jnp.einsum("rhqk,rqhe->rkhe", probs_low, attended_grad, preferred_element_type=jnp.float32).astype(jnp.bfloat16)
+    prob_grad = jnp.einsum("rqhe,rkhe->rhqk", attended_grad, value_part, preferred_element_type=jnp.float32)
+    inner_term = jnp.sum(prob_grad * probs, axis=-1, keepdims=True)
+    score_grad = (probs * (prob_grad - inner_term)).astype(jnp.bfloat16)
+    score_scale = 1.0 / math.sqrt(HDIM)
+    query_grad = (jnp.einsum("rhqk,rkhe->rqhe", score_grad, key_part, preferred_element_type=jnp.float32) * score_scale).astype(jnp.bfloat16).reshape(total_rows, width)
+    key_grad = (jnp.einsum("rhqk,rqhe->rkhe", score_grad, query_part, preferred_element_type=jnp.float32) * score_scale).astype(jnp.bfloat16).reshape(total_rows, width)
+    value_flat = value_grad.reshape(total_rows, width)
+    mixed_grad = jnp.concatenate([query_grad, key_grad, value_flat], axis=1)
+    grad_bias_query = jnp.sum(query_grad.astype(jnp.float32), axis=0)
+    grad_bias_value = jnp.sum(value_flat.astype(jnp.float32), axis=0)
+    grad_w_qkv = outer_sum(normed, mixed_grad)
+    norm_one_grad = against(mixed_grad, full_qkv)
+    input_part, grad_gain_one, grad_shift_one = first_pull(norm_one_grad)
+    grad_tokens = (middle_grad + input_part).reshape(row_count, length, width)
+
+    def sides(pick):
+        a, b = to_relative(pick(0).astype(jnp.bfloat16), bits), to_relative(pick(1).astype(jnp.bfloat16), bits)
+        return halves_of(a, b, core)
+
+    def ff_pack(f):
+        def pick(s):
+            up = grad_w_up[:, f * 1536 + s * 768 : f * 1536 + s * 768 + 768].reshape(16, 48, 768)
+            down = grad_w_down[f * 1536 : f * 1536 + 1536, s * 384 : s * 384 + 384].reshape(16, 2, 48, 384)
+            return jnp.concatenate([up, down[:, 0], down[:, 1]], axis=2)
+
+        return total_pack(*sides(pick))
+
+    def attend_pack(s):
+        at = s * 384
+        return jnp.concatenate(
+            [grad_w_qkv[:, at : at + 384], grad_w_qkv[:, 768 + at : 1152 + at],
+             grad_w_qkv[:, 1536 + at : 1920 + at], grad_w_out[:, at : at + 384]], axis=1).reshape(16, 48, 1536)
+
+    sum_a, sum_b = ff_pack(0), ff_pack(1)
+    sum_one = total_pack(*sides(attend_pack))
+
+    def finish(part):
+        upper, lower = part[:24], part[24:]
+        keep, give = halves_of(upper, lower, core)
+        back = send(give, SWAP_C)
+        return halves_of(keep, back, core)
+
+    one0, one1 = finish(sum_one)
+    share_qkv = jnp.concatenate([v[:, p * 384 : p * 384 + 384] for p in range(3) for v in (one0, one1)], axis=1)
+    share_out = jnp.concatenate([one0[:, 1152:], one1[:, 1152:]], axis=1)
+    ups = [jnp.concatenate(finish(v[:, :768]), axis=1) for v in (sum_a, sum_b)]
+    share_up = jnp.stack([u.reshape(24, 16, 96) for u in ups], axis=2).reshape(24, 3072)
+
+    def long(v):
+        return jnp.concatenate([v[:, :384], v[:, 384:]], axis=0)
+
+    keep, give = halves_of(long(sum_a[:, 768:]), long(sum_b[:, 768:]), core)
+    back = send(give, SWAP_C)
+    share_down = jnp.concatenate(halves_of(keep, back, core), axis=1)
+
+    up_rows = grad_bias_up.reshape(2, 16, 96).transpose(1, 0, 2).reshape(32, 96)
+    rows32 = jnp.concatenate(
+        [v.reshape(32, 24) for v in (grad_gain_one, grad_shift_one, grad_bias_query, grad_bias_value,
+                                     grad_bias_out, grad_gain_two, grad_shift_two)]
+        + [up_rows, grad_bias_down.reshape(32, 24), jnp.zeros((32, 96), jnp.float32)], axis=1)
+    mine = lax.psum_scatter(rows32, AXES, scatter_dimension=0, tiled=True).reshape(-1)
+    pieces, at = [], 0
+    for size in VECTOR_SIZES:
+        pieces.append(mine[at : at + size])
+        at += size
+    return (output, grad_tokens, share_qkv, share_out, share_up, share_down, *pieces)
+
+
 def solution(mesh):
+    fits = dict(mesh.shape) == {"gx": 8, "gy": 4}
+    device = on_device if fits else generic_device
     return jax.shard_map(
-        on_device,
+        device,
         mesh=mesh,
         in_specs=(
             P(("gx", "gy"), None, None),

time: 847 us -> 580 us (0.68)
  waiting for transfers between devices: 523 us -> 103 us
  other arithmetic: 31.8 us -> 113 us
  starting transfers between devices: 0.57 us -> 46 us
  local copies, waits for them, and re-layouts: 49.1 us -> 89.7 us
  between operations: 15.4 us -> 3.5 us
    reduce_scatter x4 -> x0, waiting for transfers between devices: 376 us -> none  [the longest x1 142 us: on_device(): lax.psum_scatter(grad_w_down, ('gx', 'gy'), scatter_dimension=0, tiled=True)]
    all_gather x4 -> x0, waiting for transfers between devices: 144 us -> none  [the longest x1 60.3 us: collect(): lax.all_gather(w_up, ('gx', 'gy'), axis=0, tiled=True)]
    ppermute x0 -> x68, waiting for transfers between devices: none -> 103 us  [send(): return lax.ppermute(values, AXES, perm)]
    select_n x0 -> x54, other arithmetic: none -> 46.5 us  [the longest x9 20.3 us: halves_of(): jnp.where(core == 0, own, sibling)]
    ppermute x0 -> x68, starting transfers between devices: none -> 46 us  [send(): return lax.ppermute(values, AXES, perm)]
    all_gather x0 -> x1, blocking collectives: none -> 43.4 us  [on_device(): lax.all_gather(jnp.pad(vectors, (0, 96))[None], AXES, axis=0, tiled=True)]
    unnamed x2 -> x1, blocking collectives: 83.6 us -> 40.8 us
    slice x0 -> x57, local copies, waits for them, and re-layouts: none -> 31.2 us  [the longest x6 5.89 us: spread_block(): far0, far1 = (send(along_x[0:2], SWAP_Y), send(along_y[2:4], SWAP_X))]
  transfers between devices with their start and end apart: 8 -> 68, of which waited for: 7 -> 26; matrix products, arithmetic and copies ran while one was open for 17% -> 22% of each run, Pallas kernels for 0% -> 0%
where the time goes in v1:
time: 580 us; the launch traced here: 576 us
  matrix products  136 us (23%)
  other arithmetic  113 us (19%)
  waiting for transfers between devices  103 us (18%)
  local copies, waits for them, and re-layouts  89.7 us (15%)
  blocking collectives  84.2 us (15%)
  starting transfers between devices  46 us (8%)
    ppermute x68, waiting for transfers between devices, send(): return lax.ppermute(values, AXES, perm)  103 us
    ppermute x68, starting transfers between devices, send(): return lax.ppermute(values, AXES, perm)  46 us
    dot_general x4, matrix products, against(): lax.dot_general(left, matrix, (((1,), (1,)), ((), ())), preferred_element...  45.3 us
    all_gather x1, blocking collectives, on_device(): lax.all_gather(jnp.pad(vectors, (0, 96))[None], AXES, axis=0, tiled=True)  43.4 us
    unnamed x1, blocking collectives  40.8 us
    dot_general x4, matrix products, outer_sum(): lax.dot_general(left, right, (((0,), (0,)), ((), ())), preferred_element_...  28.8 us
    select_n x9, other arithmetic, halves_of(): jnp.where(core == 0, own, sibling)  20.3 us
    another operation x26, other arithmetic, to_full(): rel = jnp.stack([jnp.stack([col, along_x]), jnp.stack([along_y, far])])  18.9 us
  transfers between devices with their start and end apart: 68, of which 26 were waited for; matrix products, arithmetic and copies ran while one was open for 22% of the time, Pallas kernels for 0%

profile of v1, /device:TPU:0, one launch (start us, length us, event | category | flops | bytes accessed | tf_op | source)
XLA Modules:
  0.0 575.7 jit_solution(16125632112777211445)
XLA Ops:
  5.3 6.1 %concatenate.277 = bf16[288]{0:T(512)(128)(2,1)S(1)} concatenate(bf16[24]{0:T(256)(128)(2,1)} %param.24, bf16[24]{0:T(256)(128)(2,1)} %param.25, bf16[24]{0:T(256)(128)(2,1)} %param.26, bf16[24]{0:T(256)(128)(2,1)} %param.27, bf16[24]{0:T(256)(128)(2,1)} %param.28, bf16[24]{0:T(256)(128)(2,1)} %param.29, bf16[24]{0:T(256)(128)(2,1)} %param.30, bf16[96]{0:T(256)(128)(2,1)} %param.31, ...), dimensions={0} | concatenate | bytes 1152 | tf_op jit(solution)/shard_map/concatenate | solution.py:362
  11.5 43.4 %all-gather.1 = bf16[32,1,384]{2,1,0:T(2,128)(2,1)S(1)} all-gather(bf16[1,1,384]{2,1,0:T(2,128)(2,1)S(1)} %reshape.711), channel_id=2, replica_groups=mesh['gx'=8,'gy'=4] {'gx','gy'}, dimensions={0}, use_global_device_ids=true | all-gather | bytes 25344 | tf_op jit(solution)/shard_map/all_gather | solution.py:365
  57.8 4.3 collective-permute-start.1
  63.8 2.6 collective-permute-done.3
  66.8 5.4 collective-permute-done.2
  73.8 2.0 collective-permute-done.17
  75.9 5.3 collective-permute-start.29
  81.2 9.5 %collective-permute-done.16 = bf16[1,48,1536]{2,1,0:T(8,128)(2,1)S(1)} collective-permute-done((bf16[1,48,1536]{2,1,0:T(8,128)(2,1)S(1)}, bf16[1,48,1536]{2,1,0:T(8,128)(2,1)S(1)}, u32[]{:S(2)}, u32[]{:S(2)}) %collective-permute-start.16) | collective-permute-done | bytes 147488 | tf_op jit(solution)/shard_map/ppermute | solution.py:282
  91.9 4.7 collective-permute-done.29
  96.6 2.0 collective-permute-done.28
  104.9 1.8 fusion.20
  107.7 2.1 collective-permute-start.7
  110.7 9.3 %collective-permute-done.18 = bf16[4,48,1536]{2,1,0:T(8,128)(2,1)} collective-permute-done((bf16[4,48,1536]{2,1,0:T(8,128)(2,1)}, bf16[4,48,1536]{2,1,0:T(8,128)(2,1)}, u32[]{:S(2)}, u32[]{:S(2)}) %collective-permute-start.18) | collective-permute-done | bytes 589856 | tf_op jit(solution)/shard_map/ppermute | solution.py:282
  124.4 8.2 %collective-permute-done.31 = bf16[4,48,1536]{2,1,0:T(8,128)(2,1)} collective-permute-done((bf16[4,48,1536]{2,1,0:T(8,128)(2,1)}, bf16[4,48,1536]{2,1,0:T(8,128)(2,1)}, u32[]{:S(2)}, u32[]{:S(2)}) %collective-permute-start.31) | collective-permute-done | bytes 589856 | tf_op jit(solution)/shard_map/ppermute | solution.py:282
  134.8 4.1 collective-permute-done.7
  159.4 2.3 collective-permute-done.24
  172.3 2.7 select_bitcast_fusion.1
  175.1 4.4 select_bitcast_fusion.3
  195.2 3.3 broadcast_select_fusion
  202.2 3.8 fusion.147
  207.4 2.3 fusion.12
  209.7 2.6 copy.194
  212.3 3.9 reshape.647
  216.1 2.6 copy.195
  218.7 3.9 reshape.648
  222.6 2.6 copy.193
  225.1 3.9 reshape.646
  229.0 4.3 fusion.10
  233.3 3.2 exponential_reduce_fusion
  237.8 5.4 fusion.27
  254.5 9.9 %fusion.42 = f32[1024,3072]{1,0:T(8,128)} fusion(bf16[768,768]{1,0:T(8,128)(2,1)S(1)} %bitcast.498, bf16[768,768]{1,0:T(8,128)(2,1)S(1)} %bitcast.496, bf16[768,768]{1,0:T(8,128)(2,1)S(1)} %bitcast.502, bf16[768,768]{1,0:T(8,128)(2,1)S(1)} %bitcast.500, f32[1024,768]{1,0:T(8,128)S(1)} %get-tuple-element.227, f32[768]{0:T(1024)S(1)} %reshape.690, ...), kind=kOutput, calls=%fused_computation.190 | convolution fusion | flops 4854644736 | bytes 20461568 | tf_op jit(solution)/shard_map/dot_general | solution.py:437
  264.3 12.2 %fusion.96 = bf16[3072,768]{1,0:T(8,128)(2,1)} fusion(bf16[1024,768]{1,0:T(8,128)(2,1)S(1)} %bitcast.446, f32[1024,3072]{1,0:T(8,128)} %fusion.42, f32[3072]{0:T(1024)S(1)} %copy-done.57), kind=kOutput, calls=%fused_computation.374 | convolution fusion | flops 4863295488 | bytes 18886656 | tf_op jit(solution)/shard_map/dot_general | solution.py:32
  276.6 30.2 %convert_reduce_fusion = (f32[3072]{0:T(1024)}, bf16[1024,3072]{1,0:T(8,128)(2,1)}) fusion(f32[1024,3072]{1,0:T(8,128)} %fusion.42, f32[3072]{0:T(1024)S(1)} %copy-done.57, bf16[1024,768]{1,0:T(8,128)(2,1)S(1)} %bitcast.447, bf16[1536,384]{1,0:T(8,128)(2,1)S(1)} %bitcast.506, bf16[1536,384]{1,0:T(8,128)(2,1)S(1)} %bitcast.504, ...), kind=kOutput, calls=%fused_computation.14 | convolution fusion | flops 4923061248 | bytes 25190400 | tf_op jit(solution)/shard_map/dot_general | solution.py:38
  306.7 9.0 %multiply_reduce_fusion.1 = (f32[768]{0:T(1024)}, f32[1024]{0:T(1024)S(1)}, f32[768]{0:T(1024)}, f32[1024,768]{1,0:T(8,128)S(1)}) fusion(f32[1024,768]{1,0:T(8,128)S(1)} %get-tuple-element.227, f32[1024]{0:T(1024)S(1)} %fusion.78, f32[1024]{0:T(1024)S(1)} %broadcast_multiply_fusion, f32[768]{0:T(1024)S(1)} %reshape.689, ...), kind=kOutput, calls=%fused_computation.75 | convolution fusion | flops 4857000960 | bytes 17323008 | tf_op jit(solution)/shard_map/dot_general | solution.py:38
  315.8 9.9 %convolution_convert_fusion = bf16[768,3072]{1,0:T(8,128)(2,1)} fusion(bf16[1024,3072]{1,0:T(8,128)(2,1)} %get-tuple-element.237, f32[1024,768]{1,0:T(8,128)S(1)} %get-tuple-element.227, f32[768]{0:T(1024)S(1)} %reshape.690, f32[768]{0:T(1024)S(1)} %reshape.689, f32[1024]{0:T(1024)S(1)} %fusion.78, f32[1024]{0:T(1024)S(1)} %broadcast_multiply_fusion), kind=kOutput, calls=%fused_computation.23 | convolution fusion | flops 4838129664 | bytes 14170112 | tf_op jit(solution)/shard_map/dot_general | solution.py:32
  329.0 2.4 convolution_convert_fusion.5
  334.9 8.6 %convert_reduce_fusion.4 = (f32[12,64]{1,0:T(8,128)}, bf16[4,256,12,64]{1,3,2,0:T(8,128)(2,1)S(1)}) fusion(f32[4,12,256,256]{2,3,1,0:T(8,128)} %copy-done, f32[4,12,256]{2,1,0:T(8,128)S(1)} %log_add_fusion, pred[4,256,256]{1,2,0:T(8,128)(4,1)S(1)} %or_and_fusion, bf16[4,256,12,64]{1,0,3,2:T(4,128)(2,1)S(1)} %reshape.664), kind=kOutput, calls=%fused_computation.77 | convolution fusion | flops 417594624 | bytes 16043008 | tf_op jit(solution)/shard_map/rhqk,rqhe->rkhe/dot_general | solution.py:459
  343.4 10.3 %multiply_reduce_fusion = (f32[4,12,256]{2,1,0:T(8,128)S(1)}, f32[4,12,256,256]{2,3,1,0:T(8,128)}) fusion(f32[4,12,256,256]{2,3,1,0:T(8,128)} %copy-done, f32[4,12,256]{2,1,0:T(8,128)S(1)} %log_add_fusion, pred[4,256,256]{1,2,0:T(8,128)(4,1)S(1)} %or_and_fusion, bf16[4,256,12,64]{1,0,3,2:T(4,128)(2,1)S(1)} %copy-done.9, ...), kind=kOutput, calls=%fused_computation.16 | convolution fusion | flops 418369536 | bytes 28672000 | tf_op jit(solution)/shard_map/rqhe,rkhe->rhqk/dot_general | solution.py:460
  353.8 7.5 %multiply_convert_fusion = bf16[4,12,256,256]{2,3,1,0:T(8,128)(2,1)S(1)} fusion(f32[4,12,256,256]{2,3,1,0:T(8,128)} %get-tuple-element.230, f32[4,12,256,256]{2,3,1,0:T(8,128)S(1)} %bitcast.445, f32[4,12,256]{2,1,0:T(8,128)S(1)} %get-tuple-element.229, f32[4,12,256]{2,1,0:T(8,128)S(1)} %log_add_fusion, pred[4,256,256]{1,2,0:T(8,128)(4,1)S(1)} %or_and_fusion), kind=kLoop, calls=%fused_computation.15 | loop fusion | flops 18874368 | bytes 31817728 | tf_op jit(solution)/shard_map/convert_element_type | solution.py:462
  361.3 2.0 fusion.30
  365.5 14.7 %add_convert_fusion = bf16[1024,768]{1,0:T(8,128)(2,1)} fusion(f32[1024,768]{1,0:T(8,128)S(1)} %copy-done.8, f32[768]{0:T(1024)S(1)} %copy-done.61, bf16[1536,384]{1,0:T(8,128)(2,1)} %bitcast.507, bf16[1536,384]{1,0:T(8,128)(2,1)S(1)} %bitcast.505, bf16[1536,384]{1,0:T(8,128)(2,1)} %bitcast.511, bf16[1536,384]{1,0:T(8,128)(2,1)} %bitcast.509, ...), kind=kOutput, calls=%fused_computation.84 | convolution fusion | flops 4884529152 | bytes 22035456 | tf_op jit(solution)/shard_map/dot_general | solution.py:440
  380.3 2.8 fusion.101
  396.4 4.2 broadcast_select_fusion.3
  401.0 4.4 broadcast_select_fusion.7
  410.4 4.3 convolution_convert_fusion.1
  420.2 4.5 broadcast_select_fusion.5
  425.2 4.6 fusion.97
  432.2 2.8 add_add_fusion.2
  435.9 40.8 %all-reduce.1 = f32[32,384]{1,0:T(8,128)S(1)} all-reduce(f32[32,384]{1,0:T(8,128)S(1)} %concatenate.359), channel_id=3, replica_groups=mesh['gx'=8,'gy'=4] {'gx','gy'}, use_global_device_ids=true, to_apply=%region_20.21.clone | all-reduce | flops 12288 | bytes 98304
  479.4 2.3 collective-permute-start.50
  489.4 1.8 collective-permute-start.41
  492.4 7.0 %collective-permute-done.53 = bf16[2,2,48,1536]{3,2,1,0:T(8,128)(2,1)S(1)} collective-permute-done((bf16[2,2,48,1536]{3,2,1,0:T(8,128)(2,1)S(1)}, bf16[2,2,48,1536]{3,2,1,0:T(8,128)(2,1)S(1)}, u32[]{:S(2)}, u32[]{:S(2)}) %collective-permute-start.53) | collective-permute-done | bytes 589856 | tf_op jit(solution)/shard_map/ppermute | solution.py:282
  500.9 11.1 %collective-permute-done.62 = bf16[2,2,48,1536]{3,2,1,0:T(8,128)(2,1)S(1)} collective-permute-done((bf16[2,2,48,1536]{3,2,1,0:T(8,128)(2,1)S(1)}, bf16[2,2,48,1536]{3,2,1,0:T(8,128)(2,1)S(1)}, u32[]{:S(2)}, u32[]{:S(2)}) %collective-permute-start.62) | collective-permute-done | bytes 589856 | tf_op jit(solution)/shard_map/ppermute | solution.py:282
  513.3 8.0 %collective-permute-done.44 = bf16[2,2,48,1536]{3,2,1,0:T(8,128)(2,1)S(1)} collective-permute-done((bf16[2,2,48,1536]{3,2,1,0:T(8,128)(2,1)S(1)}, bf16[2,2,48,1536]{3,2,1,0:T(8,128)(2,1)S(1)}, u32[]{:S(2)}, u32[]{:S(2)}) %collective-permute-start.44) | collective-permute-done | bytes 589856 | tf_op jit(solution)/shard_map/ppermute | solution.py:282
  524.5 3.1 collective-permute-done.54
  529.1 2.3 collective-permute-start.56
  531.3 2.5 collective-permute-done.63
  543.4 4.8 collective-permute-done.60
  551.0 3.9 collective-permute-done.42
  555.0 2.4 collective-permute-start.52
  559.0 1.9 collective-permute-start.47
  560.9 4.1 collective-permute-done.52
  565.1 2.1 collective-permute-start.43
  567.2 2.9 collective-permute-done.61
  (511 shorter events, 165.0 us)
Async XLA Ops:
  1.7 60.4 %collective-permute-start.14 = (bf16[96,384]{1,0:T(8,128)(2,1)S(1)}, bf16[96,384]{1,0:T(8,128)(2,1)S(1)}, u32[]{:S(2)}, u32[]{:S(2)}) collective-permute-start(bf16[96,384]{1,0:T(8,128)(2,1)S(1)} %broadcast_select_fusion.12), channel_id=1, source_target_pairs={{0,1},{1,0},{2,3},{3,2},{4,5},{5,4},{6,7},{7,6},{8,9},{9,8},{10,11... | collective-permute-start | bytes 221192 | tf_op jit(solution)/shard_map/ppermute | solution.py:282
  3.2 54.5 %collective-permute-start = (bf16[24,1536]{1,0:T(8,128)(2,1)S(1)}, bf16[24,1536]{1,0:T(8,128)(2,1)S(1)}, u32[]{:S(2)}, u32[]{:S(2)}) collective-permute-start(bf16[24,1536]{1,0:T(8,128)(2,1)S(1)} %get-tuple-element.193), channel_id=1, source_target_pairs={{0,1},{1,0},{2,3},{3,2},{4,5},{5,4},{6,7},{7,6},{8,9},{9,8},{10,11... | collective-permute-start | bytes 221192 | tf_op jit(solution)/shard_map/ppermute | solution.py:282
  4.7 52.9 %collective-permute-start.27 = (bf16[24,768]{1,0:T(8,128)(2,1)S(1)}, bf16[24,768]{1,0:T(8,128)(2,1)S(1)}, u32[]{:S(2)}, u32[]{:S(2)}) collective-permute-start(bf16[24,768]{1,0:T(8,128)(2,1)S(1)} %get-tuple-element.190), channel_id=1, source_target_pairs={{0,1},{1,0},{2,3},{3,2},{4,5},{5,4},{6,7},{7,6},{8,9},{9,8},{10,11... | collective-permute-start | bytes 110600 | tf_op jit(solution)/shard_map/ppermute | solution.py:282
  5.2 52.4 %collective-permute-start.13 = (bf16[24,768]{1,0:T(8,128)(2,1)S(1)}, bf16[24,768]{1,0:T(8,128)(2,1)S(1)}, u32[]{:S(2)}, u32[]{:S(2)}) collective-permute-start(bf16[24,768]{1,0:T(8,128)(2,1)S(1)} %get-tuple-element.191), channel_id=1, source_target_pairs={{0,1},{1,0},{2,3},{3,2},{4,5},{5,4},{6,7},{7,6},{8,9},{9,8},{10,11... | collective-permute-start | bytes 110600 | tf_op jit(solution)/shard_map/ppermute | solution.py:282
  57.7 8.7 %collective-permute-start.3 = (bf16[1,48,1536]{2,1,0:T(8,128)(2,1)S(1)}, bf16[1,48,1536]{2,1,0:T(8,128)(2,1)S(1)}, u32[]{:S(2)}, u32[]{:S(2)}) collective-permute-start(bf16[1,48,1536]{2,1,0:T(8,128)(2,1)S(1)} %maximum_select_fusion.23), channel_id=1, source_target_pairs={{0,24},{1,25},{2,26},{3,27},{4,28},{5,29},{6,30},{7,31},{8,16},{9,... | collective-permute-start | bytes 442376 | tf_op jit(solution)/shard_map/ppermute | solution.py:282
  57.8 14.4 %collective-permute-start.2 = (bf16[1,48,1536]{2,1,0:T(8,128)(2,1)S(1)}, bf16[1,48,1536]{2,1,0:T(8,128)(2,1)S(1)}, u32[]{:S(2)}, u32[]{:S(2)}) collective-permute-start(bf16[1,48,1536]{2,1,0:T(8,128)(2,1)S(1)} %maximum_select_fusion.23), channel_id=1, source_target_pairs={{0,16},{1,17},{2,18},{3,19},{4,20},{5,21},{6,22},{7,23},{8,24},{9,... | collective-permute-start | bytes 442376 | tf_op jit(solution)/shard_map/ppermute | solution.py:282
  57.8 14.3 %collective-permute-start.1 = (bf16[1,48,1536]{2,1,0:T(8,128)(2,1)S(1)}, bf16[1,48,1536]{2,1,0:T(8,128)(2,1)S(1)}, u32[]{:S(2)}, u32[]{:S(2)}) collective-permute-start(bf16[1,48,1536]{2,1,0:T(8,128)(2,1)S(1)} %maximum_select_fusion.23), channel_id=1, source_target_pairs={{0,8},{1,9},{2,10},{3,11},{4,12},{5,13},{6,14},{7,15},{8,0},{9,1},... | collective-permute-start | bytes 442376 | tf_op jit(solution)/shard_map/ppermute | solution.py:282
  62.2 13.7 %collective-permute-start.17 = (bf16[1,48,1536]{2,1,0:T(8,128)(2,1)S(1)}, bf16[1,48,1536]{2,1,0:T(8,128)(2,1)S(1)}, u32[]{:S(2)}, u32[]{:S(2)}) collective-permute-start(bf16[1,48,1536]{2,1,0:T(8,128)(2,1)S(1)} %maximum_bitcast_fusion.18), channel_id=1, source_target_pairs={{0,24},{1,25},{2,26},{3,27},{4,28},{5,29},{6,30},{7,31},{8,16},{9,... | collective-permute-start | bytes 442376 | tf_op jit(solution)/shard_map/ppermute | solution.py:282
  62.4 28.4 %collective-permute-start.16 = (bf16[1,48,1536]{2,1,0:T(8,128)(2,1)S(1)}, bf16[1,48,1536]{2,1,0:T(8,128)(2,1)S(1)}, u32[]{:S(2)}, u32[]{:S(2)}) collective-permute-start(bf16[1,48,1536]{2,1,0:T(8,128)(2,1)S(1)} %maximum_bitcast_fusion.18), channel_id=1, source_target_pairs={{0,16},{1,17},{2,18},{3,19},{4,20},{5,21},{6,22},{7,23},{8,24},{9,... | collective-permute-start | bytes 442376 | tf_op jit(solution)/shard_map/ppermute | solution.py:282
  66.4 24.4 %collective-permute-start.15 = (bf16[1,48,1536]{2,1,0:T(8,128)(2,1)S(1)}, bf16[1,48,1536]{2,1,0:T(8,128)(2,1)S(1)}, u32[]{:S(2)}, u32[]{:S(2)}) collective-permute-start(bf16[1,48,1536]{2,1,0:T(8,128)(2,1)S(1)} %maximum_bitcast_fusion.18), channel_id=1, source_target_pairs={{0,8},{1,9},{2,10},{3,11},{4,12},{5,13},{6,14},{7,15},{8,0},{9,1},... | collective-permute-start | bytes 442376 | tf_op jit(solution)/shard_map/ppermute | solution.py:282
  73.3 26.5 %collective-permute-start.5 = (bf16[4,48,1536]{2,1,0:T(8,128)(2,1)}, bf16[4,48,1536]{2,1,0:T(8,128)(2,1)}, u32[]{:S(2)}, u32[]{:S(2)}) collective-permute-start(bf16[4,48,1536]{2,1,0:T(8,128)(2,1)} %get-tuple-element.163), channel_id=1, source_target_pairs={{0,4},{1,5},{2,6},{3,7},{4,0},{5,1},{6,2},{7,3},{8,12},{9,13},{10,... | collective-permute-start | bytes 1769480 | tf_op jit(solution)/shard_map/ppermute | solution.py:282
  73.3 18.6 %collective-permute-start.30 = (bf16[1,48,1536]{2,1,0:T(8,128)(2,1)S(1)}, bf16[1,48,1536]{2,1,0:T(8,128)(2,1)S(1)}, u32[]{:S(2)}, u32[]{:S(2)}) collective-permute-start(bf16[1,48,1536]{2,1,0:T(8,128)(2,1)S(1)} %maximum_bitcast_fusion.19), channel_id=1, source_target_pairs={{0,24},{1,25},{2,26},{3,27},{4,28},{5,29},{6,30},{7,31},{8,16},{9,... | collective-permute-start | bytes 442376 | tf_op jit(solution)/shard_map/ppermute | solution.py:282
  75.9 20.7 %collective-permute-start.29 = (bf16[1,48,1536]{2,1,0:T(8,128)(2,1)S(1)}, bf16[1,48,1536]{2,1,0:T(8,128)(2,1)S(1)}, u32[]{:S(2)}, u32[]{:S(2)}) collective-permute-start(bf16[1,48,1536]{2,1,0:T(8,128)(2,1)S(1)} %maximum_bitcast_fusion.19), channel_id=1, source_target_pairs={{0,16},{1,17},{2,18},{3,19},{4,20},{5,21},{6,22},{7,23},{8,24},{9,... | collective-permute-start | bytes 442376 | tf_op jit(solution)/shard_map/ppermute | solution.py:282
  90.8 7.9 %collective-permute-start.28 = (bf16[1,48,1536]{2,1,0:T(8,128)(2,1)S(1)}, bf16[1,48,1536]{2,1,0:T(8,128)(2,1)S(1)}, u32[]{:S(2)}, u32[]{:S(2)}) collective-permute-start(bf16[1,48,1536]{2,1,0:T(8,128)(2,1)S(1)} %maximum_bitcast_fusion.19), channel_id=1, source_target_pairs={{0,8},{1,9},{2,10},{3,11},{4,12},{5,13},{6,14},{7,15},{8,0},{9,1},... | collective-permute-start | bytes 442376 | tf_op jit(solution)/shard_map/ppermute | solution.py:282
  90.8 16.9 %collective-permute-start.4 = (bf16[4,48,1536]{2,1,0:T(8,128)(2,1)}, bf16[4,48,1536]{2,1,0:T(8,128)(2,1)}, u32[]{:S(2)}, u32[]{:S(2)}) collective-permute-start(bf16[4,48,1536]{2,1,0:T(8,128)(2,1)} %get-tuple-element.163), channel_id=1, source_target_pairs={{0,2},{1,3},{2,0},{3,1},{4,6},{5,7},{6,4},{7,5},{8,10},{9,11},{10,... | collective-permute-start | bytes 1769480 | tf_op jit(solution)/shard_map/ppermute | solution.py:282
  91.9 30.4 %collective-permute-start.19 = (bf16[4,48,1536]{2,1,0:T(8,128)(2,1)}, bf16[4,48,1536]{2,1,0:T(8,128)(2,1)}, u32[]{:S(2)}, u32[]{:S(2)}) collective-permute-start(bf16[4,48,1536]{2,1,0:T(8,128)(2,1)} %get-tuple-element.159), channel_id=1, source_target_pairs={{0,4},{1,5},{2,6},{3,7},{4,0},{5,1},{6,2},{7,3},{8,12},{9,13},{10,... | collective-permute-start | bytes 1769480 | tf_op jit(solution)/shard_map/ppermute | solution.py:282
  96.6 23.4 %collective-permute-start.18 = (bf16[4,48,1536]{2,1,0:T(8,128)(2,1)}, bf16[4,48,1536]{2,1,0:T(8,128)(2,1)}, u32[]{:S(2)}, u32[]{:S(2)}) collective-permute-start(bf16[4,48,1536]{2,1,0:T(8,128)(2,1)} %get-tuple-element.159), channel_id=1, source_target_pairs={{0,2},{1,3},{2,0},{3,1},{4,6},{5,7},{6,4},{7,5},{8,10},{9,11},{10,... | collective-permute-start | bytes 1769480 | tf_op jit(solution)/shard_map/ppermute | solution.py:282
  99.7 23.6 %collective-permute-start.32 = (bf16[4,48,1536]{2,1,0:T(8,128)(2,1)}, bf16[4,48,1536]{2,1,0:T(8,128)(2,1)}, u32[]{:S(2)}, u32[]{:S(2)}) collective-permute-start(bf16[4,48,1536]{2,1,0:T(8,128)(2,1)} %get-tuple-element.161), channel_id=1, source_target_pairs={{0,4},{1,5},{2,6},{3,7},{4,0},{5,1},{6,2},{7,3},{8,12},{9,13},{10,... | collective-permute-start | bytes 1769480 | tf_op jit(solution)/shard_map/ppermute | solution.py:282
  99.7 32.9 %collective-permute-start.31 = (bf16[4,48,1536]{2,1,0:T(8,128)(2,1)}, bf16[4,48,1536]{2,1,0:T(8,128)(2,1)}, u32[]{:S(2)}, u32[]{:S(2)}) collective-permute-start(bf16[4,48,1536]{2,1,0:T(8,128)(2,1)} %get-tuple-element.161), channel_id=1, source_target_pairs={{0,2},{1,3},{2,0},{3,1},{4,6},{5,7},{6,4},{7,5},{8,10},{9,11},{10,... | collective-permute-start | bytes 1769480 | tf_op jit(solution)/shard_map/ppermute | solution.py:282
  107.7 31.3 %collective-permute-start.7 = (bf16[2,48,1536]{2,1,0:T(8,128)(2,1)S(1)}, bf16[2,48,1536]{2,1,0:T(8,128)(2,1)}, u32[]{:S(2)}, u32[]{:S(2)}) collective-permute-start(bf16[2,48,1536]{2,1,0:T(8,128)(2,1)S(1)} %slice.1049), channel_id=1, source_target_pairs={{0,2},{1,3},{2,0},{3,1},{4,6},{5,7},{6,4},{7,5},{8,10},{9,11},{10,... | collective-permute-start | bytes 884744 | tf_op jit(solution)/shard_map/ppermute | solution.py:282
  120.0 19.0 %collective-permute-start.6 = (bf16[2,48,1536]{2,1,0:T(8,128)(2,1)S(1)}, bf16[2,48,1536]{2,1,0:T(8,128)(2,1)}, u32[]{:S(2)}, u32[]{:S(2)}) collective-permute-start(bf16[2,48,1536]{2,1,0:T(8,128)(2,1)S(1)} %slice.1048), channel_id=1, source_target_pairs={{0,4},{1,5},{2,6},{3,7},{4,0},{5,1},{6,2},{7,3},{8,12},{9,13},{10,... | collective-permute-start | bytes 884744 | tf_op jit(solution)/shard_map/ppermute | solution.py:282
  122.3 31.2 %collective-permute-start.35 = (bf16[4,48,1536]{2,1,0:T(8,128)(2,1)}, bf16[4,48,1536]{2,1,0:T(8,128)(2,1)S(1)}, u32[]{:S(2)}, u32[]{:S(2)}) collective-permute-start(bf16[4,48,1536]{2,1,0:T(8,128)(2,1)} %get-tuple-element.161), channel_id=1, source_target_pairs={{0,1},{1,0},{2,3},{3,2},{4,5},{5,4},{6,7},{7,6},{8,9},{9,8},{10,11... | collective-permute-start | bytes 1769480 | tf_op jit(solution)/shard_map/ppermute | solution.py:282
  123.3 21.9 %collective-permute-start.21 = (bf16[2,48,1536]{2,1,0:T(8,128)(2,1)S(1)}, bf16[2,48,1536]{2,1,0:T(8,128)(2,1)}, u32[]{:S(2)}, u32[]{:S(2)}) collective-permute-start(bf16[2,48,1536]{2,1,0:T(8,128)(2,1)S(1)} %slice.1083), channel_id=1, source_target_pairs={{0,2},{1,3},{2,0},{3,1},{4,6},{5,7},{6,4},{7,5},{8,10},{9,11},{10,... | collective-permute-start | bytes 884744 | tf_op jit(solution)/shard_map/ppermute | solution.py:282
  132.6 12.6 %collective-permute-start.20 = (bf16[2,48,1536]{2,1,0:T(8,128)(2,1)S(1)}, bf16[2,48,1536]{2,1,0:T(8,128)(2,1)}, u32[]{:S(2)}, u32[]{:S(2)}) collective-permute-start(bf16[2,48,1536]{2,1,0:T(8,128)(2,1)S(1)} %slice.1082), channel_id=1, source_target_pairs={{0,4},{1,5},{2,6},{3,7},{4,0},{5,1},{6,2},{7,3},{8,12},{9,13},{10,... | collective-permute-start | bytes 884744 | tf_op jit(solution)/shard_map/ppermute | solution.py:282
  138.9 10.4 %collective-permute-start.34 = (bf16[2,48,1536]{2,1,0:T(8,128)(2,1)S(1)}, bf16[2,48,1536]{2,1,0:T(8,128)(2,1)S(1)}, u32[]{:S(2)}, u32[]{:S(2)}) collective-permute-start(bf16[2,48,1536]{2,1,0:T(8,128)(2,1)S(1)} %slice.1103), channel_id=1, source_target_pairs={{0,2},{1,3},{2,0},{3,1},{4,6},{5,7},{6,4},{7,5},{8,10},{9,11},{10,... | collective-permute-start | bytes 884744 | tf_op jit(solution)/shard_map/ppermute | solution.py:282
  139.0 10.4 %collective-permute-start.33 = (bf16[2,48,1536]{2,1,0:T(8,128)(2,1)S(1)}, bf16[2,48,1536]{2,1,0:T(8,128)(2,1)S(1)}, u32[]{:S(2)}, u32[]{:S(2)}) collective-permute-start(bf16[2,48,1536]{2,1,0:T(8,128)(2,1)S(1)} %slice.1102), channel_id=1, source_target_pairs={{0,4},{1,5},{2,6},{3,7},{4,0},{5,1},{6,2},{7,3},{8,12},{9,13},{10,... | collective-permute-start | bytes 884744 | tf_op jit(solution)/shard_map/ppermute | solution.py:282
  145.3 7.6 %collective-permute-start.37 = (bf16[4,48,1536]{2,1,0:T(8,128)(2,1)}, bf16[4,48,1536]{2,1,0:T(8,128)(2,1)S(1)}, u32[]{:S(2)}, u32[]{:S(2)}) collective-permute-start(bf16[4,48,1536]{2,1,0:T(8,128)(2,1)} %collective-permute-done.32), channel_id=1, source_target_pairs={{0,1},{1,0},{2,3},{3,2},{4,5},{5,4},{6,7},{7,6},{8,9},{9,8},{10,11... | collective-permute-start | bytes 1769480 | tf_op jit(solution)/shard_map/ppermute | solution.py:282
  145.3 8.4 %collective-permute-start.36 = (bf16[4,48,1536]{2,1,0:T(8,128)(2,1)}, bf16[4,48,1536]{2,1,0:T(8,128)(2,1)S(1)}, u32[]{:S(2)}, u32[]{:S(2)}) collective-permute-start(bf16[4,48,1536]{2,1,0:T(8,128)(2,1)} %collective-permute-done.31), channel_id=1, source_target_pairs={{0,1},{1,0},{2,3},{3,2},{4,5},{5,4},{6,7},{7,6},{8,9},{9,8},{10,11... | collective-permute-start | bytes 1769480 | tf_op jit(solution)/shard_map/ppermute | solution.py:282
  152.3 39.4 %collective-permute-start.8 = (bf16[4,48,1536]{2,1,0:T(8,128)(2,1)}, bf16[4,48,1536]{2,1,0:T(8,128)(2,1)S(1)}, u32[]{:S(2)}, u32[]{:S(2)}) collective-permute-start(bf16[4,48,1536]{2,1,0:T(8,128)(2,1)} %get-tuple-element.163), channel_id=1, source_target_pairs={{0,1},{1,0},{2,3},{3,2},{4,5},{5,4},{6,7},{7,6},{8,9},{9,8},{10,11... | collective-permute-start | bytes 1769480 | tf_op jit(solution)/shard_map/ppermute | solution.py:282
  152.7 10.4 %collective-permute-start.22 = (bf16[4,48,1536]{2,1,0:T(8,128)(2,1)}, bf16[4,48,1536]{2,1,0:T(8,128)(2,1)}, u32[]{:S(2)}, u32[]{:S(2)}) collective-permute-start(bf16[4,48,1536]{2,1,0:T(8,128)(2,1)} %get-tuple-element.159), channel_id=1, source_target_pairs={{0,1},{1,0},{2,3},{3,2},{4,5},{5,4},{6,7},{7,6},{8,9},{9,8},{10,11... | collective-permute-start | bytes 1769480 | tf_op jit(solution)/shard_map/ppermute | solution.py:282
  152.9 30.5 %collective-permute-start.10 = (bf16[4,48,1536]{2,1,0:T(8,128)(2,1)}, bf16[4,48,1536]{2,1,0:T(8,128)(2,1)}, u32[]{:S(2)}, u32[]{:S(2)}) collective-permute-start(bf16[4,48,1536]{2,1,0:T(8,128)(2,1)} %collective-permute-done.5), channel_id=1, source_target_pairs={{0,1},{1,0},{2,3},{3,2},{4,5},{5,4},{6,7},{7,6},{8,9},{9,8},{10,11... | collective-permute-start | bytes 1769480 | tf_op jit(solution)/shard_map/ppermute | solution.py:282
  153.5 5.1 collective-permute-start.26
  153.7 5.1 collective-permute-start.25
  158.6 33.1 %collective-permute-start.9 = (bf16[4,48,1536]{2,1,0:T(8,128)(2,1)}, bf16[4,48,1536]{2,1,0:T(8,128)(2,1)}, u32[]{:S(2)}, u32[]{:S(2)}) collective-permute-start(bf16[4,48,1536]{2,1,0:T(8,128)(2,1)} %collective-permute-done.4), channel_id=1, source_target_pairs={{0,1},{1,0},{2,3},{3,2},{4,5},{5,4},{6,7},{7,6},{8,9},{9,8},{10,11... | collective-permute-start | bytes 1769480 | tf_op jit(solution)/shard_map/ppermute | solution.py:282
  158.8 2.9 collective-permute-start.24
  161.7 2.2 collective-permute-start.23
  163.2 16.4 %collective-permute-start.12 = (bf16[2,48,1536]{2,1,0:T(8,128)(2,1)}, bf16[2,48,1536]{2,1,0:T(8,128)(2,1)}, u32[]{:S(2)}, u32[]{:S(2)}) collective-permute-start(bf16[2,48,1536]{2,1,0:T(8,128)(2,1)} %collective-permute-done.7), channel_id=1, source_target_pairs={{0,1},{1,0},{2,3},{3,2},{4,5},{5,4},{6,7},{7,6},{8,9},{9,8},{10,11... | collective-permute-start | bytes 884744 | tf_op jit(solution)/shard_map/ppermute | solution.py:282
  163.9 15.6 %collective-permute-start.11 = (bf16[2,48,1536]{2,1,0:T(8,128)(2,1)}, bf16[2,48,1536]{2,1,0:T(8,128)(2,1)}, u32[]{:S(2)}, u32[]{:S(2)}) collective-permute-start(bf16[2,48,1536]{2,1,0:T(8,128)(2,1)} %collective-permute-done.6), channel_id=1, source_target_pairs={{0,1},{1,0},{2,3},{3,2},{4,5},{5,4},{6,7},{7,6},{8,9},{9,8},{10,11... | collective-permute-start | bytes 884744 | tf_op jit(solution)/shard_map/ppermute | solution.py:282
  400.6 77.3 %collective-permute-start.49 = (bf16[2,2,4,48,1536]{4,3,2,1,0:T(8,128)(2,1)}, bf16[2,2,4,48,1536]{4,3,2,1,0:T(8,128)(2,1)}, u32[]{:S(2)}, u32[]{:S(2)}) collective-permute-start(bf16[2,2,4,48,1536]{4,3,2,1,0:T(8,128)(2,1)} %get-tuple-element.27), channel_id=1, source_target_pairs={{0,1},{1,0},{2,3},{3,2},{4,5},{5,4},{6,7},{7,6},{8,9},{9,8},{10,11... | collective-permute-start | bytes 7077896 | tf_op jit(solution)/shard_map/ppermute | solution.py:282
  405.4 78.2 %collective-permute-start.58 = (bf16[2,2,4,48,1536]{4,3,2,1,0:T(8,128)(2,1)}, bf16[2,2,4,48,1536]{4,3,2,1,0:T(8,128)(2,1)}, u32[]{:S(2)}, u32[]{:S(2)}) collective-permute-start(bf16[2,2,4,48,1536]{4,3,2,1,0:T(8,128)(2,1)} %get-tuple-element.29), channel_id=1, source_target_pairs={{0,1},{1,0},{2,3},{3,2},{4,5},{5,4},{6,7},{7,6},{8,9},{9,8},{10,11... | collective-permute-start | bytes 7077896 | tf_op jit(solution)/shard_map/ppermute | solution.py:282
  424.7 63.5 %collective-permute-start.40 = (bf16[2,2,4,48,1536]{4,3,2,1,0:T(8,128)(2,1)}, bf16[2,2,4,48,1536]{4,3,2,1,0:T(8,128)(2,1)}, u32[]{:S(2)}, u32[]{:S(2)}) collective-permute-start(bf16[2,2,4,48,1536]{4,3,2,1,0:T(8,128)(2,1)} %get-tuple-element.31), channel_id=1, source_target_pairs={{0,1},{1,0},{2,3},{3,2},{4,5},{5,4},{6,7},{7,6},{8,9},{9,8},{10,11... | collective-permute-start | bytes 7077896 | tf_op jit(solution)/shard_map/ppermute | solution.py:282
  479.4 43.9 %collective-permute-start.50 = (bf16[2,2,48,1536]{3,2,1,0:T(8,128)(2,1)S(1)}, bf16[2,2,48,1536]{3,2,1,0:T(8,128)(2,1)S(1)}, u32[]{:S(2)}, u32[]{:S(2)}) collective-permute-start(bf16[2,2,48,1536]{3,2,1,0:T(8,128)(2,1)S(1)} %fusion.45), channel_id=1, source_target_pairs={{0,2},{1,3},{2,0},{3,1},{4,6},{5,7},{6,4},{7,5},{8,10},{9,11},{10,... | collective-permute-start | bytes 1769480 | tf_op jit(solution)/shard_map/ppermute | solution.py:282
  483.1 16.3 %collective-permute-start.53 = (bf16[2,2,48,1536]{3,2,1,0:T(8,128)(2,1)S(1)}, bf16[2,2,48,1536]{3,2,1,0:T(8,128)(2,1)S(1)}, u32[]{:S(2)}, u32[]{:S(2)}) collective-permute-start(bf16[2,2,48,1536]{3,2,1,0:T(8,128)(2,1)S(1)} %fusion.46), channel_id=1, source_target_pairs={{0,4},{1,5},{2,6},{3,7},{4,0},{5,1},{6,2},{7,3},{8,12},{9,13},{10,... | collective-permute-start | bytes 1769480 | tf_op jit(solution)/shard_map/ppermute | solution.py:282
  485.0 44.1 %collective-permute-start.59 = (bf16[2,2,48,1536]{3,2,1,0:T(8,128)(2,1)S(1)}, bf16[2,2,48,1536]{3,2,1,0:T(8,128)(2,1)S(1)}, u32[]{:S(2)}, u32[]{:S(2)}) collective-permute-start(bf16[2,2,48,1536]{3,2,1,0:T(8,128)(2,1)S(1)} %fusion.47), channel_id=1, source_target_pairs={{0,2},{1,3},{2,0},{3,1},{4,6},{5,7},{6,4},{7,5},{8,10},{9,11},{10,... | collective-permute-start | bytes 1769480 | tf_op jit(solution)/shard_map/ppermute | solution.py:282
  487.9 24.1 %collective-permute-start.62 = (bf16[2,2,48,1536]{3,2,1,0:T(8,128)(2,1)S(1)}, bf16[2,2,48,1536]{3,2,1,0:T(8,128)(2,1)S(1)}, u32[]{:S(2)}, u32[]{:S(2)}) collective-permute-start(bf16[2,2,48,1536]{3,2,1,0:T(8,128)(2,1)S(1)} %fusion.48), channel_id=1, source_target_pairs={{0,4},{1,5},{2,6},{3,7},{4,0},{5,1},{6,2},{7,3},{8,12},{9,13},{10,... | collective-permute-start | bytes 1769480 | tf_op jit(solution)/shard_map/ppermute | solution.py:282
  489.4 47.4 %collective-permute-start.41 = (bf16[2,2,48,1536]{3,2,1,0:T(8,128)(2,1)S(1)}, bf16[2,2,48,1536]{3,2,1,0:T(8,128)(2,1)S(1)}, u32[]{:S(2)}, u32[]{:S(2)}) collective-permute-start(bf16[2,2,48,1536]{3,2,1,0:T(8,128)(2,1)S(1)} %fusion.43), channel_id=1, source_target_pairs={{0,2},{1,3},{2,0},{3,1},{4,6},{5,7},{6,4},{7,5},{8,10},{9,11},{10,... | collective-permute-start | bytes 1769480 | tf_op jit(solution)/shard_map/ppermute | solution.py:282
  499.4 21.9 %collective-permute-start.44 = (bf16[2,2,48,1536]{3,2,1,0:T(8,128)(2,1)S(1)}, bf16[2,2,48,1536]{3,2,1,0:T(8,128)(2,1)S(1)}, u32[]{:S(2)}, u32[]{:S(2)}) collective-permute-start(bf16[2,2,48,1536]{3,2,1,0:T(8,128)(2,1)S(1)} %fusion.44), channel_id=1, source_target_pairs={{0,4},{1,5},{2,6},{3,7},{4,0},{5,1},{6,2},{7,3},{8,12},{9,13},{10,... | collective-permute-start | bytes 1769480 | tf_op jit(solution)/shard_map/ppermute | solution.py:282
  512.1 15.5 %collective-permute-start.54 = (bf16[2,48,1536]{2,1,0:T(8,128)(2,1)S(1)}, bf16[2,48,1536]{2,1,0:T(8,128)(2,1)S(1)}, u32[]{:S(2)}, u32[]{:S(2)}) collective-permute-start(bf16[2,48,1536]{2,1,0:T(8,128)(2,1)S(1)} %fusion.54), channel_id=1, source_target_pairs={{0,2},{1,3},{2,0},{3,1},{4,6},{5,7},{6,4},{7,5},{8,10},{9,11},{10,... | collective-permute-start | bytes 884744 | tf_op jit(solution)/shard_map/ppermute | solution.py:282
  521.3 12.6 %collective-permute-start.63 = (bf16[2,48,1536]{2,1,0:T(8,128)(2,1)S(1)}, bf16[2,48,1536]{2,1,0:T(8,128)(2,1)S(1)}, u32[]{:S(2)}, u32[]{:S(2)}) collective-permute-start(bf16[2,48,1536]{2,1,0:T(8,128)(2,1)S(1)} %fusion.49), channel_id=1, source_target_pairs={{0,2},{1,3},{2,0},{3,1},{4,6},{5,7},{6,4},{7,5},{8,10},{9,11},{10,... | collective-permute-start | bytes 884744 | tf_op jit(solution)/shard_map/ppermute | solution.py:282
  523.4 14.7 %collective-permute-start.45 = (bf16[2,48,1536]{2,1,0:T(8,128)(2,1)S(1)}, bf16[2,48,1536]{2,1,0:T(8,128)(2,1)S(1)}, u32[]{:S(2)}, u32[]{:S(2)}) collective-permute-start(bf16[2,48,1536]{2,1,0:T(8,128)(2,1)S(1)} %fusion.59), channel_id=1, source_target_pairs={{0,2},{1,3},{2,0},{3,1},{4,6},{5,7},{6,4},{7,5},{8,10},{9,11},{10,... | collective-permute-start | bytes 884744 | tf_op jit(solution)/shard_map/ppermute | solution.py:282
  528.9 29.6 %collective-permute-start.55 = (bf16[48,1536]{1,0:T(8,128)(2,1)S(1)}, bf16[48,1536]{1,0:T(8,128)(2,1)S(1)}, u32[]{:S(2)}, u32[]{:S(2)}) collective-permute-start(bf16[48,1536]{1,0:T(8,128)(2,1)S(1)} %get-tuple-element.176), channel_id=1, source_target_pairs={{0,16},{1,17},{2,18},{3,19},{4,20},{5,21},{6,22},{7,23},{8,24},{9,... | collective-permute-start | bytes 442376 | tf_op jit(solution)/shard_map/ppermute | solution.py:282
  529.1 30.0 %collective-permute-start.56 = (bf16[48,1536]{1,0:T(8,128)(2,1)S(1)}, bf16[48,1536]{1,0:T(8,128)(2,1)S(1)}, u32[]{:S(2)}, u32[]{:S(2)}) collective-permute-start(bf16[48,1536]{1,0:T(8,128)(2,1)S(1)} %get-tuple-element.177), channel_id=1, source_target_pairs={{0,24},{1,25},{2,26},{3,27},{4,28},{5,29},{6,30},{7,31},{8,16},{9,... | collective-permute-start | bytes 442376 | tf_op jit(solution)/shard_map/ppermute | solution.py:282
  533.9 7.0 %collective-permute-start.51 = (bf16[2,48,1536]{2,1,0:T(8,128)(2,1)S(1)}, bf16[2,48,1536]{2,1,0:T(8,128)(2,1)S(1)}, u32[]{:S(2)}, u32[]{:S(2)}) collective-permute-start(bf16[2,48,1536]{2,1,0:T(8,128)(2,1)S(1)} %get-tuple-element.41), channel_id=1, source_target_pairs={{0,4},{1,5},{2,6},{3,7},{4,0},{5,1},{6,2},{7,3},{8,12},{9,13},{10,... | collective-permute-start | bytes 884744 | tf_op jit(solution)/shard_map/ppermute | solution.py:282
  536.9 28.3 %collective-permute-start.64 = (bf16[48,1536]{1,0:T(8,128)(2,1)S(1)}, bf16[48,1536]{1,0:T(8,128)(2,1)S(1)}, u32[]{:S(2)}, u32[]{:S(2)}) collective-permute-start(bf16[48,1536]{1,0:T(8,128)(2,1)S(1)} %get-tuple-element.178), channel_id=1, source_target_pairs={{0,16},{1,17},{2,18},{3,19},{4,20},{5,21},{6,22},{7,23},{8,24},{9,... | collective-permute-start | bytes 442376 | tf_op jit(solution)/shard_map/ppermute | solution.py:282
  538.0 29.2 %collective-permute-start.65 = (bf16[48,1536]{1,0:T(8,128)(2,1)S(1)}, bf16[48,1536]{1,0:T(8,128)(2,1)S(1)}, u32[]{:S(2)}, u32[]{:S(2)}) collective-permute-start(bf16[48,1536]{1,0:T(8,128)(2,1)S(1)} %get-tuple-element.179), channel_id=1, source_target_pairs={{0,24},{1,25},{2,26},{3,27},{4,28},{5,29},{6,30},{7,31},{8,16},{9,... | collective-permute-start | bytes 442376 | tf_op jit(solution)/shard_map/ppermute | solution.py:282
  540.9 7.3 %collective-permute-start.60 = (bf16[2,48,1536]{2,1,0:T(8,128)(2,1)S(1)}, bf16[2,48,1536]{2,1,0:T(8,128)(2,1)S(1)}, u32[]{:S(2)}, u32[]{:S(2)}) collective-permute-start(bf16[2,48,1536]{2,1,0:T(8,128)(2,1)S(1)} %get-tuple-element.51), channel_id=1, source_target_pairs={{0,4},{1,5},{2,6},{3,7},{4,0},{5,1},{6,2},{7,3},{8,12},{9,13},{10,... | collective-permute-start | bytes 884744 | tf_op jit(solution)/shard_map/ppermute | solution.py:282
  548.3 6.7 %collective-permute-start.42 = (bf16[2,48,1536]{2,1,0:T(8,128)(2,1)S(1)}, bf16[2,48,1536]{2,1,0:T(8,128)(2,1)S(1)}, u32[]{:S(2)}, u32[]{:S(2)}) collective-permute-start(bf16[2,48,1536]{2,1,0:T(8,128)(2,1)S(1)} %get-tuple-element.53), channel_id=1, source_target_pairs={{0,4},{1,5},{2,6},{3,7},{4,0},{5,1},{6,2},{7,3},{8,12},{9,13},{10,... | collective-permute-start | bytes 884744 | tf_op jit(solution)/shard_map/ppermute | solution.py:282
  555.0 10.0 %collective-permute-start.52 = (bf16[48,1536]{1,0:T(8,128)(2,1)S(1)}, bf16[48,1536]{1,0:T(8,128)(2,1)S(1)}, u32[]{:S(2)}, u32[]{:S(2)}) collective-permute-start(bf16[48,1536]{1,0:T(8,128)(2,1)S(1)} %fusion.74), channel_id=1, source_target_pairs={{0,8},{1,9},{2,10},{3,11},{4,12},{5,13},{6,14},{7,15},{8,0},{9,1},... | collective-permute-start | bytes 442376 | tf_op jit(solution)/shard_map/ppermute | solution.py:282
  558.5 12.4 %collective-permute-start.46 = (bf16[48,1536]{1,0:T(8,128)(2,1)S(1)}, bf16[48,1536]{1,0:T(8,128)(2,1)S(1)}, u32[]{:S(2)}, u32[]{:S(2)}) collective-permute-start(bf16[48,1536]{1,0:T(8,128)(2,1)S(1)} %get-tuple-element.180), channel_id=1, source_target_pairs={{0,16},{1,17},{2,18},{3,19},{4,20},{5,21},{6,22},{7,23},{8,24},{9,... | collective-permute-start | bytes 442376 | tf_op jit(solution)/shard_map/ppermute | solution.py:282
  559.0 12.0 %collective-permute-start.47 = (bf16[48,1536]{1,0:T(8,128)(2,1)S(1)}, bf16[48,1536]{1,0:T(8,128)(2,1)S(1)}, u32[]{:S(2)}, u32[]{:S(2)}) collective-permute-start(bf16[48,1536]{1,0:T(8,128)(2,1)S(1)} %get-tuple-element.181), channel_id=1, source_target_pairs={{0,24},{1,25},{2,26},{3,27},{4,28},{5,29},{6,30},{7,31},{8,16},{9,... | collective-permute-start | bytes 442376 | tf_op jit(solution)/shard_map/ppermute | solution.py:282
  565.0 5.1 collective-permute-start.61
  565.1 6.6 %collective-permute-start.43 = (bf16[48,1536]{1,0:T(8,128)(2,1)S(1)}, bf16[48,1536]{1,0:T(8,128)(2,1)S(1)}, u32[]{:S(2)}, u32[]{:S(2)}) collective-permute-start(bf16[48,1536]{1,0:T(8,128)(2,1)S(1)} %fusion.73), channel_id=1, source_target_pairs={{0,8},{1,9},{2,10},{3,11},{4,12},{5,13},{6,14},{7,15},{8,0},{9,1},... | collective-permute-start | bytes 442376 | tf_op jit(solution)/shard_map/ppermute | solution.py:282
  570.9 3.1 collective-permute-start.67
  571.8 2.0 collective-permute-start.48
  (74 other events, 779.2 us)
